TPU v7x, 32 devices: a whole 2x2x4 slice. The times are simulated.
32 devices in a mesh: gx: 2 (over y), gy: 4 (over x, core), gz: 4 (over z).
Axes of the slice: x: 2, y: 2, z: 4, core: 2. Of those that a mesh axis runs over, the one named last changes fastest.
Arguments:
- density: float32 [8, 256, 512], P('gx', 'gy', 'gz'), may hold values from 0.18 to 1
- fixed_mask: int32 [8, 256, 512], P('gx', 'gy', 'gz'), may hold values 0 or 1
- load_mask: int32 [8, 256, 512], P('gx', 'gy', 'gz'), may hold values 0 or 1
- load_values: float32 [3, 8, 256, 512], P(None, 'gx', 'gy', 'gz'), may hold values from -7.5 to 7.5
Outputs:
- filtered: float32 [8, 256, 512], P('gx', 'gy', 'gz')
- displacement: float32 [3, 8, 256, 512], P(None, 'gx', 'gy', 'gz')
- residual: float32 [3, 8, 256, 512], P(None, 'gx', 'gy', 'gz')
All inputs are finite; a program needn't handle non-finite values. No bound on the sum of `fixed_mask` or of `load_mask` on one device may be relied on, other than what follows from the above.
Results may differ from a plain program's by a relative error of at most 0.00035.
Values sent between devices are 32-bit elements; how exact they have to be, the bound alone decides.
No kernel may reach another device: no remote copies, remote signals or barrier semaphores. Data moves between devices by JAX's collectives and lax.ppermute only.
A program may use at most 128 MiB of HBM per device.

v0:
```python
import jax
import jax.numpy as jnp
import numpy as np
from jax import lax
from jax.sharding import PartitionSpec as P

FILTER_ITERS = 2
SOLVE_ITERS = 4


MIN_MODULUS = 0.001
filter_weight = 0.75


def passed_along(value, axis, steps):
    count = lax.axis_size(axis)
    initial, last = (max(0, -steps), min(count, count - steps))
    return lax.ppermute(value, axis, [(source, source + steps) for source in range(initial, last)])


def padded_2(block, sides, width):
    for axis, dim in sides:
        count = lax.axis_size(axis)
        forward = [(i, i + 1) for i in range(count - 1)]
        backward = [(target, source) for source, target in forward]
        low = lax.ppermute(
            lax.slice_in_dim(block, block.shape[dim] - width, None, axis=dim), axis, forward
        )
        high = lax.ppermute(lax.slice_in_dim(block, 0, width, axis=dim), axis, backward)
        block = jnp.concatenate([low, block, high], axis=dim)
    return block


def element_table():
    poisson = 0.3
    lame_first = poisson / ((1.0 + poisson) * (1.0 - 2.0 * poisson))
    lame_shear = 1.0 / (2.0 * (1.0 + poisson))
    elastic = np.zeros((6, 6))
    elastic[:3, :3] = lame_first
    for index in range(3):
        elastic[index, index] += 2.0 * lame_shear
        elastic[index + 3, index + 3] = lame_shear
    gauss_value = 1.0 / np.sqrt(3.0)
    matrix = np.zeros((24, 24))
    for first in (-gauss_value, gauss_value):
        for second in (-gauss_value, gauss_value):
            for third in (-gauss_value, gauss_value):
                gauss_point = (first, second, third)
                strain = np.zeros((6, 24))
                for corner in range(8):
                    corner_signs = [
                        2 * (corner >> 2 & 1) - 1,
                        2 * (corner >> 1 & 1) - 1,
                        2 * (corner & 1) - 1,
                    ]
                    factors = [1.0 + corner_signs[d] * gauss_point[d] for d in range(3)]
                    slopes = [
                        corner_signs[d] * factors[(d + 1) % 3] * factors[(d + 2) % 3] / 4.0
                        for d in range(3)
                    ]
                    column = 3 * corner
                    strain[0, column] = slopes[0]
                    strain[1, column + 1] = slopes[1]
                    strain[2, column + 2] = slopes[2]
                    strain[3, column] = slopes[1]
                    strain[3, column + 1] = slopes[0]
                    strain[4, column + 1] = slopes[2]
                    strain[4, column + 2] = slopes[1]
                    strain[5, column] = slopes[2]
                    strain[5, column + 2] = slopes[0]
                matrix += strain.T @ elastic @ strain / 8.0
    return matrix.reshape(8, 3, 8, 3).transpose(0, 2, 1, 3)


def corner_offsets(corner):
    return (corner >> 2 & 1, corner >> 1 & 1, corner & 1)


def apply_stiffness(disp_pad, mod_pad, extent):
    stiffness = jnp.asarray(element_table(), jnp.float32)
    size_x, size_y, size_z = extent
    result = jnp.zeros((3, size_x, size_y, size_z), jnp.float32)
    for corner_a in range(8):
        offs_a = corner_offsets(corner_a)
        moduli_part = mod_pad[
            1 - offs_a[0] : 1 - offs_a[0] + size_x,
            1 - offs_a[1] : 1 - offs_a[1] + size_y,
            1 - offs_a[2] : 1 - offs_a[2] + size_z,
        ]
        inner_sum = jnp.zeros((3, size_x, size_y, size_z), jnp.float32)
        for corner_b in range(8):
            offs_b = corner_offsets(corner_b)
            start_x = 1 - offs_a[0] + offs_b[0]
            start_y = 1 - offs_a[1] + offs_b[1]
            start_z = 1 - offs_a[2] + offs_b[2]
            shifted = disp_pad[
                :,
                start_x : start_x + size_x,
                start_y : start_y + size_y,
                start_z : start_z + size_z,
            ]
            for comp in range(3):
                inner_sum = (
                    inner_sum
                    + stiffness[corner_a, corner_b, :, comp][:, None, None, None]
                    * shifted[comp][None]
                )
        result = result + moduli_part[None] * inner_sum
    return result


def jacobi_diagonal(mod_pad, extent):
    stiffness = jnp.asarray(element_table(), jnp.float32)
    size_x, size_y, size_z = extent
    diagonal = jnp.zeros((3, size_x, size_y, size_z), jnp.float32)
    for corner_a in range(8):
        offs_a = corner_offsets(corner_a)
        moduli_part = mod_pad[
            1 - offs_a[0] : 1 - offs_a[0] + size_x,
            1 - offs_a[1] : 1 - offs_a[1] + size_y,
            1 - offs_a[2] : 1 - offs_a[2] + size_z,
        ]
        block_diag = jnp.stack([stiffness[corner_a, corner_a, comp, comp] for comp in range(3)])
        diagonal = diagonal + moduli_part[None] * block_diag[:, None, None, None]
    return diagonal


def face_sum(padded):
    beside = padded[2:, 1:-1, 1:-1] + padded[:-2, 1:-1, 1:-1]
    beside = beside + padded[1:-1, 2:, 1:-1] + padded[1:-1, :-2, 1:-1]
    return beside + padded[1:-1, 1:-1, 2:] + padded[1:-1, 1:-1, :-2]


def edge_count(global_index, total):
    return (global_index > 0).astype(jnp.float32) + (global_index < total - 1).astype(jnp.float32)


def neighbour_counts(extent):
    size_x, size_y, size_z = extent
    index_x = lax.axis_index("gx") * size_x + jnp.arange(size_x, dtype=jnp.int32)
    index_y = lax.axis_index("gy") * size_y + jnp.arange(size_y, dtype=jnp.int32)
    index_z = lax.axis_index("gz") * size_z + jnp.arange(size_z, dtype=jnp.int32)
    count_x = edge_count(index_x, size_x * lax.axis_size("gx"))
    count_y = edge_count(index_y, size_y * lax.axis_size("gy"))
    count_z = edge_count(index_z, size_z * lax.axis_size("gz"))
    return count_x[:, None, None] + count_y[None, :, None] + count_z[None, None, :]


def lower_moduli(moduli):
    rim_x = passed_along(moduli[-1:], "gx", 1)
    extended = jnp.concatenate([rim_x, moduli], axis=0)
    rim_y = passed_along(extended[:, -1:], "gy", 1)
    extended = jnp.concatenate([rim_y, extended], axis=1)
    rim_z = passed_along(extended[:, :, -1:], "gz", 1)
    return jnp.concatenate([rim_z, extended], axis=2)


def displacement_halo(field):
    return padded_2(field, (("gx", 1), ("gy", 2), ("gz", 3)), 1)


def residual_dot(first, second):
    return lax.psum(jnp.sum(first * second), ("gx", "gy", "gz"))


def curvature_dot(first, second):
    return lax.psum(jnp.sum(first * second), ("gx", "gy", "gz"))


def conjugate(operator, precond, force, iters):
    iterate = jnp.zeros_like(force)
    residual = force
    search = precond(residual)
    direction = search
    res_dot = residual_dot(residual, search)
    for iteration in range(iters):
        image = operator(direction)
        step_size = res_dot / curvature_dot(direction, image)
        iterate = iterate + step_size * direction
        residual = residual - step_size * image
        if iteration + 1 < iters:
            search = precond(residual)
            new_dot = residual_dot(residual, search)
            direction = search + new_dot / res_dot * direction
            res_dot = new_dot
    return (iterate, residual)


def shards(density, fixed_mask, load_mask, load_values):
    extent = density.shape
    counts = neighbour_counts(extent)

    def filter_apply(field):
        padded = padded_2(field, (("gx", 0), ("gy", 1), ("gz", 2)), 1)
        return field + filter_weight * (counts * field - face_sum(padded))

    def identity(field):
        return field

    filtered, unused = conjugate(filter_apply, identity, density, FILTER_ITERS)
    moduli = MIN_MODULUS + (1.0 - MIN_MODULUS) * filtered * filtered * jnp.abs(filtered)
    mod_pad = lower_moduli(moduli)
    free_nodes = (1 - fixed_mask).astype(jnp.float32)
    force = free_nodes[None] * load_mask.astype(jnp.float32)[None] * load_values
    inverse_diag = free_nodes[None] / jacobi_diagonal(mod_pad, extent)

    def elastic_apply(field):
        return free_nodes[None] * apply_stiffness(displacement_halo(field), mod_pad, extent)

    def jacobi(field):
        return inverse_diag * field

    displacement, residual = conjugate(elastic_apply, jacobi, force, SOLVE_ITERS)
    return (filtered, displacement, residual)


def solution(mesh):
    return jax.shard_map(
        shards,
        mesh=mesh,
        in_specs=(
            P("gx", "gy", "gz"),
            P("gx", "gy", "gz"),
            P("gx", "gy", "gz"),
            P(None, "gx", "gy", "gz"),
        ),
        out_specs=(P("gx", "gy", "gz"), P(None, "gx", "gy", "gz"), P(None, "gx", "gy", "gz")),
        check_vma=False,
    )
```

profile of v0, /device:TPU:0, one launch (start us, length us, event | category | flops | bytes accessed | tf_op | source)
XLA Modules:
  0.0 1043.6 jit_solution(7331890099792246726)
XLA Ops:
  2.8 4.9 collective-permute-start.1
  12.9 4.5 collective-permute-done.2
  18.8 4.6 collective-permute-start.5
  28.9 42.0 %all-reduce.1 = (f32[]{:T(128)}, f32[]{:T(128)}) all-reduce(f32[]{:T(128)} %get-tuple-element.9, f32[]{:T(128)} %get-tuple-element.8), channel_id=1, replica_groups=mesh['gx'=2,'gy'=4,'gz'=4] {'gx','gy','gz'}, use_global_device_ids=true, to_apply=%region_1.0 | all-reduce | flops 2 | bytes 16 | tf_op jit(solution)/shard_map/psum | solution.py:163
  72.9 40.9 %psum.86 = f32[]{:T(128)} all-reduce(f32[]{:T(128)} %multiply_reduce_fusion.5), channel_id=1, replica_groups=mesh['gx'=2,'gy'=4,'gz'=4] {'gx','gy','gz'}, use_global_device_ids=true, to_apply=%region_5.0 | all-reduce | flops 1 | bytes 8 | tf_op jit(solution)/shard_map/psum | solution.py:163
  115.2 4.4 collective-permute-start.7
  121.2 4.2 collective-permute-done.6
  128.0 3.0 collective-permute-done.8
  132.6 4.6 collective-permute-start.11
  142.7 40.4 %psum.87 = f32[]{:T(128)} all-reduce(f32[]{:T(128)} %fusion.380), channel_id=1, replica_groups=mesh['gx'=2,'gy'=4,'gz'=4] {'gx','gy','gz'}, use_global_device_ids=true, to_apply=%region_7.0 | all-reduce | flops 1 | bytes 8 | tf_op jit(solution)/shard_map/psum | solution.py:167
  185.1 4.4 collective-permute-start.12
  195.8 4.3 collective-permute-done.14
  201.4 4.2 collective-permute-start.15
  208.6 4.1 collective-permute-done.16
  214.1 3.0 collective-permute-start.17
  223.2 4.9 collective-permute-start.20
  232.2 3.1 slice_bitcast_fusion.215
  235.3 4.3 slice_bitcast_fusion.202
  239.6 3.2 slice_bitcast_fusion.203
  317.1 11.9 %multiply_reduce_fusion.3 = (f32[]{:T(128)}, f32[]{:T(128)}, f32[3,4,64,128]{3,2,1,0:T(8,128)S(1)}) fusion(f32[3,4,64,128]{3,2,1,0:T(8,128)S(1)} %copy-done.13, f32[4,64,128]{2,1,0:T(8,128)S(1)} %get-tuple-element.431, f32[4,64,128]{2,1,0:T(8,128)} %copy.126, f32[4,64,128]{2,1,0:T(8,128)} %copy.125, f32[4,64,128]{2,1,0:T(8,128)} %copy.124, ...), kind=kLoop, calls=%fused_computation.501 | loop fusion | flops 37945344 | bytes 12846216 | tf_op jit(solution)/shard_map/reduce_sum | solution.py:167
  329.0 40.2 %all-reduce = (f32[]{:T(128)}, f32[]{:T(128)}) all-reduce(f32[]{:T(128)} %get-tuple-element.7, f32[]{:T(128)} %get-tuple-element.6), channel_id=1, replica_groups=mesh['gx'=2,'gy'=4,'gz'=4] {'gx','gy','gz'}, use_global_device_ids=true, to_apply=%region_9.0 | all-reduce | flops 2 | bytes 16 | tf_op jit(solution)/shard_map/psum | solution.py:163
  371.3 41.4 %psum.90 = f32[]{:T(128)} all-reduce(f32[]{:T(128)} %get-tuple-element.24), channel_id=1, replica_groups=mesh['gx'=2,'gy'=4,'gz'=4] {'gx','gy','gz'}, use_global_device_ids=true, to_apply=%region_13.0 | all-reduce | flops 1 | bytes 8 | tf_op jit(solution)/shard_map/psum | solution.py:163
  415.1 4.3 collective-permute-start.21
  421.7 4.3 collective-permute-done.22
  427.4 3.0 collective-permute-start.23
  438.6 5.0 collective-permute-start.26
  448.8 3.4 slice_bitcast_fusion.149
  454.7 2.9 slice_bitcast_fusion.161
  536.1 11.5 %multiply_reduce_fusion.2 = (f32[]{:T(128)}, f32[3,4,64,128]{3,2,1,0:T(8,128)S(1)}) fusion(f32[3,4,64,128]{3,2,1,0:T(8,128)S(1)} %multiply_add_fusion.71, f32[4,64,128]{2,1,0:T(8,128)} %copy.187, f32[4,64,128]{2,1,0:T(8,128)} %copy.186, f32[4,64,128]{2,1,0:T(8,128)} %copy.185, f32[4,64,128]{2,1,0:T(8,128)S(1)} %copy-done.26, f32[4,64,128]{2,1,0:T(8,128)} %copy.184, ...), kind=kLoop, calls=%fused_computation.499 | loop fusion | flops 37552128 | bytes 12584068 | tf_op jit(solution)/shard_map/reduce_sum | solution.py:167
  547.6 40.2 %psum.91 = f32[]{:T(128)} all-reduce(f32[]{:T(128)} %get-tuple-element.22), channel_id=1, replica_groups=mesh['gx'=2,'gy'=4,'gz'=4] {'gx','gy','gz'}, use_global_device_ids=true, to_apply=%region_15.0 | all-reduce | flops 1 | bytes 8 | tf_op jit(solution)/shard_map/psum | solution.py:167
  589.8 39.5 %psum.92 = f32[]{:T(128)} all-reduce(f32[]{:T(128)} %get-tuple-element.20), channel_id=1, replica_groups=mesh['gx'=2,'gy'=4,'gz'=4] {'gx','gy','gz'}, use_global_device_ids=true, to_apply=%region_17.0 | all-reduce | flops 1 | bytes 8 | tf_op jit(solution)/shard_map/psum | solution.py:163
  630.5 4.3 collective-permute-start.27
  637.0 4.3 collective-permute-done.28
  642.7 3.0 collective-permute-start.29
  656.5 4.8 collective-permute-start.32
  666.5 3.5 slice_bitcast_fusion.95
  672.6 3.2 slice_bitcast_fusion.107
  760.0 12.2 %multiply_reduce_fusion.1 = (f32[]{:T(128)}, f32[3,4,64,128]{3,2,1,0:T(8,128)S(1)}) fusion(f32[3,4,64,128]{3,2,1,0:T(8,128)S(1)} %multiply_add_fusion.47, f32[4,64,128]{2,1,0:T(8,128)} %copy.248, f32[4,64,128]{2,1,0:T(8,128)} %copy.247, f32[4,64,128]{2,1,0:T(8,128)} %copy.246, f32[4,64,128]{2,1,0:T(8,128)S(1)} %copy-done.26, f32[4,64,128]{2,1,0:T(8,128)} %copy.245, ...), kind=kLoop, calls=%fused_computation.497 | loop fusion | flops 37552128 | bytes 12584068 | tf_op jit(solution)/shard_map/reduce_sum | solution.py:167
  772.2 40.2 %psum.93 = f32[]{:T(128)} all-reduce(f32[]{:T(128)} %get-tuple-element.18), channel_id=1, replica_groups=mesh['gx'=2,'gy'=4,'gz'=4] {'gx','gy','gz'}, use_global_device_ids=true, to_apply=%region_19.0 | all-reduce | flops 1 | bytes 8 | tf_op jit(solution)/shard_map/psum | solution.py:167
  814.4 40.7 %psum.94 = f32[]{:T(128)} all-reduce(f32[]{:T(128)} %get-tuple-element.16), channel_id=1, replica_groups=mesh['gx'=2,'gy'=4,'gz'=4] {'gx','gy','gz'}, use_global_device_ids=true, to_apply=%region_21.0 | all-reduce | flops 1 | bytes 8 | tf_op jit(solution)/shard_map/psum | solution.py:163
  856.5 4.5 collective-permute-start.33
  863.2 4.3 collective-permute-done.34
  868.9 3.0 collective-permute-start.35
  882.6 4.7 collective-permute-start.38
  892.7 3.5 slice_bitcast_fusion.41
  898.7 3.3 slice_bitcast_fusion.53
  987.4 12.7 %multiply_reduce_fusion = (f32[]{:T(128)}, f32[3,4,64,128]{3,2,1,0:T(8,128)}) fusion(f32[3,4,64,128]{3,2,1,0:T(8,128)S(1)} %multiply_add_fusion.23, f32[4,64,128]{2,1,0:T(8,128)} %copy.309, f32[4,64,128]{2,1,0:T(8,128)} %copy.308, f32[4,64,128]{2,1,0:T(8,128)} %copy.307, f32[4,64,128]{2,1,0:T(8,128)S(1)} %copy-done.27, f32[4,64,128]{2,1,0:T(8,128)} %copy.306, ...), kind=kLoop, calls=%fused_computation.495 | loop fusion | flops 37552128 | bytes 12584068 | tf_op jit(solution)/shard_map/reduce_sum | solution.py:167
  1000.1 40.2 %psum.95 = f32[]{:T(128)} all-reduce(f32[]{:T(128)} %get-tuple-element.14), channel_id=1, replica_groups=mesh['gx'=2,'gy'=4,'gz'=4] {'gx','gy','gz'}, use_global_device_ids=true, to_apply=%region_23.0 | all-reduce | flops 1 | bytes 8 | tf_op jit(solution)/shard_map/psum | solution.py:167
  (566 shorter events, 438.8 us)
Async XLA Ops:
  1.5 8.7 collective-permute-start
  2.8 6.5 collective-permute-start.1
  10.2 2.7 collective-permute-start.3
  11.5 5.9 collective-permute-start.2
  17.5 8.8 collective-permute-start.4
  18.8 9.2 collective-permute-start.5
  115.2 6.0 collective-permute-start.7
  119.6 5.8 collective-permute-start.6
  125.4 2.6 collective-permute-start.9
  126.7 4.3 collective-permute-start.8
  131.1 69.2 %copy-start.77 = (s32[4,64,128]{2,1,0:T(8,128)S(1)}, s32[4,64,128]{2,1,0:T(8,128)}, u32[]{:S(2)}) copy-start(s32[4,64,128]{2,1,0:T(8,128)} %param.10) | copy-start | bytes 393220
  131.1 69.2 %copy-start.78 = (s32[4,64,128]{2,1,0:T(8,128)S(1)}, s32[4,64,128]{2,1,0:T(8,128)}, u32[]{:S(2)}) copy-start(s32[4,64,128]{2,1,0:T(8,128)} %param.11) | copy-start | bytes 393220
  131.2 8.9 collective-permute-start.10
  132.6 9.2 collective-permute-start.11
  185.1 131.9 %copy-start.10 = (f32[4,64,128]{2,1,0:T(8,128)}, f32[4,64,128]{2,1,0:T(8,128)S(1)}, u32[]{:S(2)}) copy-start(f32[4,64,128]{2,1,0:T(8,128)S(1)} %get-tuple-element.27) | copy-start | bytes 393220
  185.1 5.9 collective-permute-start.12
  191.1 2.1 collective-permute-start.13
  193.3 6.8 collective-permute-start.14
  201.3 169.3 %copy-start.6 = (f32[4,64,128]{2,1,0:T(8,128)}, f32[4,64,128]{2,1,0:T(8,128)S(1)}, u32[]{:S(2)}) copy-start(f32[4,64,128]{2,1,0:T(8,128)S(1)} %get-tuple-element.416) | copy-start | bytes 393220
  201.3 169.3 %copy-start.18 = (f32[4,64,128]{2,1,0:T(8,128)}, f32[4,64,128]{2,1,0:T(8,128)S(1)}, u32[]{:S(2)}) copy-start(f32[4,64,128]{2,1,0:T(8,128)S(1)} %get-tuple-element.431) | copy-start | bytes 393220
  201.4 7.2 collective-permute-start.15
  205.6 7.1 collective-permute-start.16
  212.8 7.7 collective-permute-start.18
  214.1 5.8 collective-permute-start.17
  221.9 7.8 collective-permute-start.19
  223.2 6.5 collective-permute-start.20
  371.3 60.1 %copy-start.21 = (f32[3,4,64,128]{3,2,1,0:T(8,128)}, f32[3,4,64,128]{3,2,1,0:T(8,128)S(1)}, u32[]{:S(2)}) copy-start(f32[3,4,64,128]{3,2,1,0:T(8,128)S(1)} %get-tuple-element.25) | copy-start | bytes 1179652
  415.1 6.5 collective-permute-start.21
  419.5 6.5 collective-permute-start.22
  426.1 7.0 collective-permute-start.24
  427.4 5.7 collective-permute-start.23
  437.1 7.5 collective-permute-start.25
  438.6 6.0 collective-permute-start.26
  536.1 52.9 %copy-start.22 = (f32[3,4,64,128]{3,2,1,0:T(8,128)S(1)}, f32[3,4,64,128]{3,2,1,0:T(8,128)}, u32[]{:S(2)}) copy-start(f32[3,4,64,128]{3,2,1,0:T(8,128)} %copy-done.21) | copy-start | bytes 1179652
  630.5 6.5 collective-permute-start.27
  634.8 6.5 collective-permute-start.28
  641.4 7.0 collective-permute-start.30
  642.7 5.8 collective-permute-start.29
  655.0 7.3 collective-permute-start.31
  656.5 5.9 collective-permute-start.32
  856.5 6.7 collective-permute-start.33
  861.0 6.5 collective-permute-start.34
  867.6 7.0 collective-permute-start.36
  868.9 5.7 collective-permute-start.35
  881.2 7.3 collective-permute-start.37
  882.6 5.9 collective-permute-start.38
  987.4 54.3 %copy-start.14 = (f32[3,4,64,128]{3,2,1,0:T(8,128)S(1)}, f32[3,4,64,128]{3,2,1,0:T(8,128)}, u32[]{:S(2)}) copy-start(f32[3,4,64,128]{3,2,1,0:T(8,128)} %param.12) | copy-start | bytes 1179652
  987.4 54.3 %copy-start.19 = (f32[4,64,128]{2,1,0:T(8,128)S(1)}, f32[4,64,128]{2,1,0:T(8,128)}, u32[]{:S(2)}) copy-start(f32[4,64,128]{2,1,0:T(8,128)} %copy-done.18) | copy-start | bytes 393220
  (87 other events, 738.8 us)
where the time goes:
time: 1060 us; the launch traced here: 1040 us
  blocking collectives  406 us (38%)
  local copies, waits for them, and re-layouts  394 us (37%)
  starting transfers between devices  102 us (10%)
  other arithmetic  76.1 us (7%)
  waiting for transfers between devices  50.6 us (5%)
  between operations  15.6 us (1%)
    mul x238, local copies, waits for them, and re-layouts, apply_stiffness(): stiffness[corner_a, corner_b, :, comp][:, None, None, None]  374 us
    psum x6, blocking collectives, residual_dot(): return lax.psum(jnp.sum(first * second), ('gx', 'gy', 'gz'))  245 us
    psum x4, blocking collectives, curvature_dot(): return lax.psum(jnp.sum(first * second), ('gx', 'gy', 'gz'))  161 us
    ppermute x18, starting transfers between devices, padded_2(): lax.ppermute(lax.slice_in_dim(block, block.shape[dim] - width, None, axis...  69.7 us
    reduce_sum x6, other arithmetic, curvature_dot(): return lax.psum(jnp.sum(first * second), ('gx', 'gy', 'gz'))  49.9 us
    ppermute x18, waiting for transfers between devices, padded_2(): lax.ppermute(lax.slice_in_dim(block, 0, width, axis=dim), axis, backward)  34.6 us
    ppermute x18, starting transfers between devices, padded_2(): lax.ppermute(lax.slice_in_dim(block, 0, width, axis=dim), axis, backward)  23.8 us
  transfers between devices with their start and end apart: 39, of which 22 were waited for; matrix products, arithmetic and copies ran while one was open for 2% of the time, Pallas kernels for 0%

commit v1 on v0

--- a/solution.py
+++ b/solution.py
@@ -1,7 +1,11 @@
+import functools
+
 import jax
 import jax.numpy as jnp
 import numpy as np
 from jax import lax
+from jax.experimental import pallas as pl
+from jax.experimental.pallas import tpu as pltpu
 from jax.sharding import PartitionSpec as P
 
 FILTER_ITERS = 2
@@ -186,7 +190,7 @@
     return (iterate, residual)
 
 
-def shards(density, fixed_mask, load_mask, load_values):
+def general_shards(density, fixed_mask, load_mask, load_values):
     extent = density.shape
     counts = neighbour_counts(extent)
 
@@ -212,6 +216,663 @@
 
     displacement, residual = conjugate(elastic_apply, jacobi, force, SOLVE_ITERS)
     return (filtered, displacement, residual)
+
+
+HALO = 4
+SW = 16
+FACE = 8
+PARTS = 8
+AXES = ("gx", "gy", "gz")
+SHIFTS = (1.2, 0.4, 2.0, 0.8)
+VMEM_LIMIT = 24 * 1024 * 1024
+POISSON = 0.3
+LAME = POISSON / ((1.0 + POISSON) * (1.0 - 2.0 * POISSON))
+SHEAR = 1.0 / (2.0 * (1.0 + POISSON))
+AXIAL = LAME + 2.0 * SHEAR
+MODES = [(a, b, g) for a in range(2) for b in range(2) for g in range(2)]
+
+
+def lanes_of(shape):
+    return lax.broadcasted_iota(jnp.int32, shape, len(shape) - 1)
+
+
+def rows_of(shape):
+    return lax.broadcasted_iota(jnp.int32, shape, len(shape) - 2)
+
+
+def turned(value, shift, axis):
+    size = value.shape[axis]
+    if isinstance(shift, int):
+        shift = shift % size
+        if shift == 0:
+            return value
+    else:
+        shift = lax.rem(shift + 4 * size, size)
+    return pltpu.roll(value, shift, axis)
+
+
+def either(flag, first, second):
+    return jnp.where(jnp.full(first.shape, flag, jnp.int32) == 0, first, second)
+
+
+def pack_kernel(density, fixed, load_mask, load_values, fields, send_a, send_b):
+    planes, rows, _ = density.shape
+    odd = lax.rem(lax.axis_index("gy"), 2)
+    for p in range(planes):
+        free = (1 - fixed[p]).astype(jnp.float32)
+        loaded = free * load_mask[p].astype(jnp.float32)
+        fields[p] = density[p]
+        fields[planes + p] = free
+        for c in range(3):
+            fields[(2 + c) * planes + p] = loaded * load_values[c, p]
+    row_a = pl.multiple_of((1 - odd) * (rows - FACE), FACE)
+    row_b = pl.multiple_of(odd * (rows - FACE), FACE)
+    send_a[...] = fields[:, pl.ds(row_a, FACE), :]
+    send_b[...] = fields[:, pl.ds(row_b, FACE), :]
+
+
+def strip_kernel(fields, from_a, from_b, density_out, node_out, own, send_a, send_b):
+    total, rows, lanes = fields.shape
+    planes = total // 5
+    odd_y = lax.rem(lax.axis_index("gy"), 2)
+    odd_z = lax.rem(lax.axis_index("gz"), 2)
+    row = rows_of((FACE, lanes))
+    for q in range(total):
+        above = either(odd_y, from_a[q], from_b[q])
+        below = either(odd_y, from_b[q], from_a[q])
+        if q < planes:
+            density_out[q, :rows] = fields[q]
+            density_out[q, rows : rows + FACE] = above
+            density_out[q, rows + FACE :] = below
+        else:
+            node_out[q - planes, :rows] = fields[q]
+            node_out[q - planes, rows:] = jnp.where(row < HALO, above, below)
+    wide = rows + 2 * FACE
+    tall = rows + FACE
+    own[:wide] = jnp.zeros((wide, lanes), jnp.float32)
+    lane = lanes_of((wide, lanes))
+    low = jnp.zeros((wide, lanes), jnp.float32)
+    high = low
+    for p in range(planes):
+        value = density_out[p]
+        base = SW * p
+        low = jnp.where((lane >= base) & (lane < base + 8), turned(value, base, 1), low)
+        high = jnp.where((lane >= base + 8) & (lane < base + 16), turned(value, base + 16, 1), high)
+    send_a[:wide] = either(odd_z, high, low)
+    send_b[:wide] = either(odd_z, low, high)
+    lane = lanes_of((tall, lanes))
+    for pair in range(2):
+        low = jnp.zeros((tall, lanes), jnp.float32)
+        high = low
+        mine = low
+        for half in range(2):
+            for p in range(planes):
+                value = node_out[(2 * pair + half) * planes + p]
+                base = SW * p + (lanes // 2) * half
+                four = turned(value, base + 4, 1)
+                twelve = turned(value, base + 12, 1)
+                part = (lane - base) // 4
+                inside = (lane >= base) & (lane < base + SW)
+                mine = jnp.where(inside & (part == 0), four, mine)
+                low = jnp.where(inside & (part == 1), four, low)
+                high = jnp.where(inside & (part == 2), twelve, high)
+                mine = jnp.where(inside & (part == 3), twelve, mine)
+        at = wide + pair * tall
+        own[at : at + tall] = mine
+        send_a[at : at + tall] = either(odd_z, high, low)
+        send_b[at : at + tall] = either(odd_z, low, high)
+
+
+def filter_kernel(grid, own, other, strip_own, strip_other, window, first, strip_v, strip_g, dots):
+    planes, wide, lanes = own.shape
+    rows = wide - 2 * FACE
+    count = 2 * planes
+    total_y, total_z = grid
+    gx = lax.axis_index("gx")
+    base_y = lax.axis_index("gy") * rows
+    base_z = lax.axis_index("gz") * lanes
+    mine = gx * planes
+    window[pl.ds(mine, planes)] = own[...]
+    window[pl.ds(planes - mine, planes)] = other[...]
+    shape = (wide, lanes)
+    lane = lanes_of(shape)
+    row = rows_of(shape)
+    lower = either(gx, strip_own[:wide], strip_other[:wide])
+    upper = either(gx, strip_other[:wide], strip_own[:wide])
+    strip_v[...] = jnp.where(lane < lanes // 2, lower, turned(upper, lanes // 2, 1))
+    at_y = base_y + jnp.where(row < rows + FACE, row, row - wide)
+    pass_y = ((at_y >= 0) & (at_y < total_y - 1)).astype(jnp.float32)
+    pass_z = (base_z + lane < total_z - 1).astype(jnp.float32)
+    back_z = (base_z + lane > 0).astype(jnp.float32)
+    place = lax.rem(lane, SW)
+    at_strip = base_z + jnp.where(place < 8, lanes + place, place - SW)
+    strip_pass = ((at_strip >= 0) & (at_strip < total_z - 1)).astype(jnp.float32)
+    strip_back = ((at_strip >= 1) & (at_strip < total_z)).astype(jnp.float32)
+
+    def along_y(value):
+        ahead = (turned(value, -1, 0) - value) * pass_y
+        return turned(ahead, 1, 0) - ahead
+
+    def laplace(source, strip, p):
+        value = source[p]
+        result = (value - source[jnp.minimum(p + 1, count - 1)]) + (value - source[jnp.maximum(p - 1, 0)])
+        result = result + along_y(value)
+        side = strip[...]
+        ahead = jnp.where(lane == lanes - 1, turned(side, lanes - 1 - SW * p, 1), turned(value, -1, 1))
+        behind = jnp.where(lane == 0, turned(side, 0 - (SW * p + SW - 1), 1), turned(value, 1, 1))
+        result = result + (value - ahead) * pass_z + (value - behind) * back_z
+        return filter_weight * result
+
+    def first_plane(p, carry):
+        first[p] = laplace(window, strip_v, p)
+        return carry
+
+    lax.fori_loop(0, count, first_plane, 0)
+    value = strip_v[...]
+    edge_low = jnp.zeros(shape, jnp.float32)
+    edge_high = edge_low
+    for p in range(count):
+        edge_low = jnp.where(lane == SW * p + SW - 1, turned(window[p], SW * p + SW - 1, 1), edge_low)
+        edge_high = jnp.where(lane == SW * p, turned(window[p], SW * p - (lanes - 1), 1), edge_high)
+    ahead = jnp.where(place == SW - 1, edge_low, turned(value, -1, 1))
+    behind = jnp.where(place == 0, edge_high, turned(value, 1, 1))
+    result = along_y(value) + (value - ahead) * strip_pass + (value - behind) * strip_back
+    ahead = jnp.where(lane < lanes - SW, turned(value, -SW, 1) - value, 0.0)
+    result = result + turned(ahead, SW, 1) - ahead
+    strip_g[...] = filter_weight * result
+
+    def add_dots(p, sums):
+        plane = mine + p
+        w = window[plane][:rows]
+        g = first[plane][:rows]
+        gg = laplace(first, strip_g, plane)[:rows]
+        terms = (w * w, w * g, g * g, g * gg)
+        return tuple(
+            s + jnp.sum(t.reshape(rows // 8, 8, lanes), axis=0) for s, t in zip(sums, terms)
+        )
+
+    zero = jnp.zeros((8, lanes), jnp.float32)
+    spread(lax.fori_loop(0, planes, add_dots, (zero,) * 4), dots)
+
+
+def spread(sums, dots):
+    lanes = dots.shape[-1]
+    lane = lanes_of((1, lanes))
+    line = jnp.zeros((1, lanes), jnp.float32)
+    for k, value in enumerate(sums):
+        value = jnp.sum(jnp.sum(value, axis=0, keepdims=True), axis=1, keepdims=True)
+        line = jnp.where(lane == k, value, line)
+    for k in range(dots.shape[0]):
+        dots[k] = line
+
+
+def gathered(dots, count):
+    line = jnp.sum(dots[...], axis=0)
+    lane = lanes_of(line.shape)
+    return [
+        jnp.sum(jnp.where(lane == k, line, 0.0), axis=1, keepdims=True) for k in range(count)
+    ]
+
+
+def element_forces(u, modulus):
+    shear = modulus * (SHEAR / 16.0)
+    shear_3 = modulus * (SHEAR / 48.0)
+    twist = modulus * ((AXIAL + 2.0 * SHEAR) / 144.0)
+    normal = modulus * (2.0 * SHEAR / 16.0)
+    paired = modulus * ((AXIAL + SHEAR) / 48.0)
+    x, y, z = u
+    f = [{}, {}, {}]
+    trace = (x[1, 0, 0] + y[0, 1, 0] + z[0, 0, 1]) * (LAME / (2.0 * SHEAR))
+    f[0][1, 0, 0] = (trace + x[1, 0, 0]) * normal
+    f[1][0, 1, 0] = (trace + y[0, 1, 0]) * normal
+    f[2][0, 0, 1] = (trace + z[0, 0, 1]) * normal
+    ratio = LAME / (AXIAL + SHEAR)
+    for (c, m), (d, n) in (
+        ((0, (1, 1, 0)), (2, (0, 1, 1))),
+        ((1, (1, 1, 0)), (2, (1, 0, 1))),
+        ((0, (1, 0, 1)), (1, (0, 1, 1))),
+    ):
+        f[c][m] = (u[c][m] + ratio * u[d][n]) * paired
+        f[d][n] = (u[d][n] + ratio * u[c][m]) * paired
+    for (c, m), (d, n) in (
+        ((0, (0, 1, 0)), (1, (1, 0, 0))),
+        ((1, (0, 0, 1)), (2, (0, 1, 0))),
+        ((0, (0, 0, 1)), (2, (1, 0, 0))),
+    ):
+        f[c][m] = f[d][n] = (u[c][m] + u[d][n]) * shear
+    three = ((0, (0, 1, 1)), (1, (1, 0, 1)), (2, (1, 1, 0)))
+    both = x[0, 1, 1] + y[1, 0, 1] + z[1, 1, 0]
+    for c, m in three:
+        f[c][m] = (both + u[c][m]) * shear_3
+    for c in range(3):
+        f[c][1, 1, 1] = u[c][1, 1, 1] * twist
+    return f
+
+
+def solve_kernel(
+    grid, diagonal, window, first, strip_v, strip_g, filter_dots, node_own, node_other, strip_own, strip_other,
+    filtered, basis, scale, dots,
+    modulus, inverse, free, fields, pairs, kept, carried, near, far,
+    s_modulus, s_inverse, s_free, s_old, s_disp, s_near, s_far, s_edge,
+):
+    count, wide, lanes = window.shape
+    rows = wide - 2 * FACE
+    tall = rows + FACE
+    tiles = tall // 8
+    planes = count // 2
+    total_y, total_z = grid
+    gx = lax.axis_index("gx")
+    base_y = lax.axis_index("gy") * rows
+    base_z = lax.axis_index("gz") * lanes
+    mine = gx * planes
+
+    a, b, c, e = gathered(filter_dots, 4)
+    step = a / (a + b)
+    beta = step * step * (c - b * b / a) / a
+    to_v = step * b / a + beta
+    to_g = -step
+    bottom = to_v * to_v * (a + b) + 2.0 * to_v * to_g * (b + c) + to_g * to_g * (c + e)
+    second = beta * a / bottom
+    weight_v = step + second * to_v
+    weight_g = second * to_g
+
+    shape = (wide, lanes)
+    lane = lanes_of(shape)
+    row = rows_of(shape)
+    at_y = base_y + jnp.where(row < rows + FACE, row, row - wide)
+    inside_y = (at_y >= 0) & (at_y < total_y)
+    place = lax.rem(lane, SW)
+    at_strip = base_z + jnp.where(place < 8, lanes + place, place - SW)
+    inside_strip = inside_y & (at_strip >= 0) & (at_strip < total_z)
+    small = rows_of((8, lanes))
+
+    def folded(value):
+        tail = jnp.where(small < HALO, value[rows : rows + 8], value[rows + 8 :])
+        return value[:rows], tail
+
+    def put(ref, index, value):
+        head, tail = folded(value)
+        ref[index, :rows] = head
+        ref[index, rows:] = tail
+
+    def moduli_of(v, g):
+        value = weight_v * v + weight_g * g
+        return value, MIN_MODULUS + (1.0 - MIN_MODULUS) * value * value * jnp.abs(value)
+
+    side = moduli_of(strip_v[...], strip_g[...])[1]
+    side = jnp.where(inside_strip, side, 0.0)
+
+    def inverted(total, open_nodes):
+        return jnp.where(total > 0.0, open_nodes / jnp.where(total > 0.0, diagonal * total, 1.0), 0.0)
+
+    node_at = [pl.ds(pl.multiple_of(mine, planes), planes), pl.ds(pl.multiple_of(planes - mine, planes), planes)]
+    for f in range(4):
+        for source, at in zip((node_own, node_other), node_at):
+            value = source[f * planes : (f + 1) * planes]
+            if f == 0:
+                free[at] = value
+            else:
+                basis[0, f - 1, at] = value
+
+    s_line = jnp.zeros(shape, jnp.float32)
+    previous = jnp.zeros(shape, jnp.float32)
+    for p in range(count):
+        value, mod = moduli_of(window[p], first[p])
+        mod = jnp.where(inside_y, mod, 0.0)
+        put(modulus, p, mod)
+        edge = turned(side, 0 - (SW * p + SW - 1), 1)
+        across = mod + jnp.where(lane == 0, edge, turned(mod, 1, 1))
+        across = across + turned(across, 1, 0)
+        head, tail = folded(across + previous)
+        previous = across
+        inverse[p, :rows] = inverted(head, free[p, :rows])
+        inverse[p, rows:] = inverted(tail, free[p, rows:])
+        s_line = jnp.where((lane >= SW * p) & (lane < SW * p + 4), turned(mod, SW * p + 4, 1), s_line)
+        s_line = jnp.where((lane >= SW * p + 12) & (lane < SW * p + 16), turned(mod, SW * p + 12, 1), s_line)
+    for p in range(planes):
+        v = window[mine + p]
+        g = first[mine + p]
+        filtered[p] = (weight_v * v + weight_g * g)[:rows]
+
+    s_mod = jnp.where(
+        (place >= 4) & (place < 8), turned(side, 4, 1), jnp.where((place >= 8) & (place < 12), turned(side, -4, 1), s_line)
+    )
+    put(s_modulus, 0, s_mod)
+    across = s_mod + jnp.where(place == 8, turned(side, -3, 1), turned(s_mod, 1, 1))
+    across = across + turned(across, 1, 0)
+    across = across + jnp.where(lane < SW, 0.0, turned(across, SW, 1))
+    s_head, s_tail = folded(across)
+
+    half = lanes // 2
+    for pair in range(2):
+        at = wide + pair * tall
+        lower = either(gx, strip_own[at : at + tall], strip_other[at : at + tall])
+        upper = either(gx, strip_other[at : at + tall], strip_own[at : at + tall])
+        left = lanes_of((tall, lanes)) < half
+        one = jnp.where(left, lower, turned(upper, half, 1))
+        two = jnp.where(left, turned(lower, half, 1), upper)
+        for k, value in ((2 * pair, one), (2 * pair + 1, two)):
+            if k == 0:
+                s_free[...] = value
+            else:
+                s_old[k - 1] = value
+    s_inverse[:rows] = inverted(s_head, s_free[:rows])
+    s_inverse[rows:] = inverted(s_tail, s_free[rows:])
+    for c in range(3):
+        s_disp[0, c, :tall] = s_inverse[...] * s_old[c]
+        s_disp[0, c, tall : tall + 1] = s_disp[0, c, 0:1]
+
+    lane = lanes_of((8, lanes))
+    last_plane = lane >= lanes - SW
+    first_plane = lane < SW
+
+    for j in range(4):
+        for t in range(tiles):
+            r = 8 * t
+            u = []
+            for c in range(3):
+                now = s_disp[j, c, r : r + 8]
+                after = s_disp[j, c, r + 1 : r + 9]
+                modes = {}
+                for beta_, value in ((0, now + after), (1, after - now)):
+                    beside = jnp.where(last_plane, 0.0, turned(value, -SW, 1))
+                    for alpha, across in ((0, value + beside), (1, beside - value)):
+                        next_z = turned(across, -1, 1)
+                        if (alpha, beta_) != (0, 0):
+                            modes[alpha, beta_, 0] = across + next_z
+                        modes[alpha, beta_, 1] = next_z - across
+                u.append(modes)
+            f = element_forces(u, s_modulus[0, r : r + 8])
+            for c in range(3):
+                for g in range(2):
+                    t_beta = []
+                    for beta_ in range(2):
+                        diff = f[c][1, beta_, g]
+                        if (beta_, g) == (0, 0):
+                            lower, upper = -diff, diff
+                        else:
+                            total = f[c][0, beta_, g]
+                            lower, upper = total - diff, total + diff
+                        t_beta.append(lower + jnp.where(first_plane, 0.0, turned(upper, SW, 1)))
+                    s_near[2 * c + g, r : r + 8] = t_beta[0] - t_beta[1]
+                    s_far[2 * c + g, r + 8 : r + 16] = t_beta[0] + t_beta[1]
+        for k in range(6):
+            s_far[k, 7:8] = s_far[k, tall + 7 : tall + 8]
+        for t in range(tiles):
+            r = 8 * t
+            for c in range(3):
+                total = s_near[2 * c, r : r + 8] + s_far[2 * c, r + 7 : r + 15]
+                diff = s_near[2 * c + 1, r : r + 8] + s_far[2 * c + 1, r + 7 : r + 15]
+                upper = total + diff
+                s_edge[j, c, r : r + 8] = upper
+                if j < 3:
+                    out = (total - diff) + turned(upper, 1, 1)
+                    new = s_free[r : r + 8] * out - SHIFTS[j] * s_old[c, r : r + 8]
+                    s_old[c, r : r + 8] = new
+                    s_disp[j + 1, c, r : r + 8] = s_inverse[r : r + 8] * new
+        if j < 3:
+            for c in range(3):
+                s_disp[j + 1, c, tall : tall + 1] = s_disp[j + 1, c, 0:1]
+
+    def spread_z(j, c, p, r, disp):
+        edge = turned(s_disp[j, c, r : r + 8], lanes - 1 - (SW * p + 4), 1)
+        ahead = jnp.where(lane == lanes - 1, edge, turned(disp, -1, 1))
+        pairs[2 * c, p, r : r + 8] = disp + ahead
+        pairs[2 * c + 1, p, r : r + 8] = ahead - disp
+
+    def close_rows(p):
+        for k in range(6):
+            pairs[k, p, tall : tall + 1] = pairs[k, p, 0:1]
+
+    for k in range(6):
+        pairs[k, count] = jnp.zeros(pairs.shape[2:], jnp.float32)
+
+    def start_plane(p, carry):
+        for t in range(tiles):
+            r = 8 * t
+            for c in range(3):
+                spread_z(0, c, p, r, inverse[p, r : r + 8] * basis[0, c, p, r : r + 8])
+        close_rows(p)
+        return carry
+
+    lax.fori_loop(0, count, start_plane, 0)
+
+    def along_rows(p, r):
+        result = []
+        for k in range(6):
+            now = pairs[k, p, r : r + 8]
+            after = pairs[k, p, r + 1 : r + 9]
+            result.append((now + after, after - now))
+        return result
+
+    for j in range(4):
+        low = gx * j
+        high = count - 1 - j + gx * (j + 1)
+        for t in range(tiles):
+            r = 8 * t
+            for k, both in enumerate(along_rows(low, r)):
+                for beta_ in range(2):
+                    kept[2 * k + beta_, r : r + 8] = both[beta_]
+                    carried[2 * k + beta_, r : r + 8] = jnp.zeros((8, lanes), jnp.float32)
+
+        def layer(p, state, j=j):
+            for t in range(tiles):
+                r = 8 * t
+                upper_rows = along_rows(p + 1, r)
+                u = []
+                for c in range(3):
+                    modes = {}
+                    for g in range(2):
+                        for beta_ in range(2):
+                            k = 2 * (2 * c + g) + beta_
+                            now = kept[k, r : r + 8]
+                            above = upper_rows[2 * c + g][beta_]
+                            if (beta_, g) != (0, 0):
+                                modes[0, beta_, g] = now + above
+                            modes[1, beta_, g] = above - now
+                            kept[k, r : r + 8] = above
+                    u.append(modes)
+                f = element_forces(u, modulus[p, r : r + 8])
+                for c in range(3):
+                    for g in range(2):
+                        t_beta = []
+                        for beta_ in range(2):
+                            k = 2 * (2 * c + g) + beta_
+                            diff = f[c][1, beta_, g]
+                            before = carried[k, r : r + 8]
+                            if (beta_, g) == (0, 0):
+                                t_beta.append(before - diff)
+                                carried[k, r : r + 8] = diff
+                            else:
+                                total = f[c][0, beta_, g]
+                                t_beta.append(before + (total - diff))
+                                carried[k, r : r + 8] = total + diff
+                        near[2 * c + g, r : r + 8] = t_beta[0] - t_beta[1]
+                        far[2 * c + g, r + 8 : r + 16] = t_beta[0] + t_beta[1]
+            for k in range(6):
+                far[k, 7:8] = far[k, tall + 7 : tall + 8]
+            for t in range(tiles):
+                r = 8 * t
+                open_nodes = free[p, r : r + 8]
+                inv = inverse[p, r : r + 8]
+                for c in range(3):
+                    total = near[2 * c, r : r + 8] + far[2 * c, r + 7 : r + 15]
+                    diff = near[2 * c + 1, r : r + 8] + far[2 * c + 1, r + 7 : r + 15]
+                    edge = turned(s_edge[j, c, r : r + 8], 0 - (SW * p + 11), 1)
+                    out = (total - diff) + jnp.where(lane == 0, edge, turned(total + diff, 1, 1))
+                    new = open_nodes * out - SHIFTS[j] * basis[j, c, p, r : r + 8]
+                    basis[j + 1, c, p, r : r + 8] = new
+                    if j < 3:
+                        spread_z(j + 1, c, p, r, inv * new)
+            if j < 3:
+                close_rows(p)
+            return state
+
+        lax.fori_loop(low, high, layer, 0)
+
+    order = [(i, k) for i in range(4) for k in range(i, 5)]
+
+    def add_dots(p, sums):
+        plane = mine + p
+        sums = list(sums)
+        for t in range(rows // 8):
+            r = 8 * t
+            inv = inverse[plane, r : r + 8]
+            scale[p, r : r + 8] = inv
+            for c in range(3):
+                ys = [basis[i, c, plane, r : r + 8] for i in range(5)]
+                ws = [inv * y for y in ys[:4]]
+                for i in range(5):
+                    fields[i, c, p, r : r + 8] = ys[i]
+                for n, (i, k) in enumerate(order):
+                    sums[n] = sums[n] + ws[i] * ys[k]
+        return tuple(sums)
+
+    zero = jnp.zeros((8, lanes), jnp.float32)
+    spread(lax.fori_loop(0, planes, add_dots, (zero,) * len(order)), dots)
+
+
+def combine_kernel(dots, basis, scale, displacement, residual):
+    order = [(i, k) for i in range(4) for k in range(i, 5)]
+    gram = {}
+    for value, (i, k) in zip(gathered(dots, len(order)), order):
+        gram[i, k] = gram[k, i] = value
+    zero = jnp.zeros((1, 1), jnp.float32)
+    one = jnp.ones((1, 1), jnp.float32)
+    res = [one]
+    search = [one]
+    disp = []
+    res_dot = gram[0, 0]
+    for iteration in range(4):
+        image = [zero] * (iteration + 2)
+        for i, value in enumerate(search):
+            image[i] = image[i] + SHIFTS[i] * value
+            image[i + 1] = image[i + 1] + value
+        curve = zero
+        for i, left in enumerate(search):
+            inner = zero
+            for k, right in enumerate(image):
+                inner = inner + gram[i, k] * right
+            curve = curve + left * inner
+        step = res_dot / curve
+        disp = [d + step * s for d, s in zip(disp + [zero], search)]
+        res = [r - step * q for r, q in zip(res + [zero], image)]
+        if iteration < 3:
+            new_dot = zero
+            for i, left in enumerate(res):
+                inner = zero
+                for k, right in enumerate(res):
+                    inner = inner + gram[i, k] * right
+                new_dot = new_dot + left * inner
+            search = [r + new_dot / res_dot * s for r, s in zip(res, search + [zero])]
+            res_dot = new_dot
+    planes, rows, lanes = scale.shape
+    disp = [jnp.broadcast_to(d, (8, lanes)) for d in disp]
+    res = [jnp.broadcast_to(r, (8, lanes)) for r in res]
+
+    def plane(p, carry):
+        for r in range(0, rows, 8):
+            inv = scale[p, r : r + 8]
+            for c in range(3):
+                ys = [basis[i, c, p, r : r + 8] for i in range(5)]
+                first = disp[0] * ys[0]
+                second = res[0] * ys[0]
+                for i in range(1, 5):
+                    second = second + res[i] * ys[i]
+                    if i < 4:
+                        first = first + disp[i] * ys[i]
+                displacement[c, p, r : r + 8] = inv * first
+                residual[c, p, r : r + 8] = second
+        return carry
+
+    lax.fori_loop(0, planes, plane, 0)
+
+
+def call(kernel, outs, *args, scratch=()):
+    f32 = lambda shape: jax.ShapeDtypeStruct(shape, jnp.float32)
+    return pl.pallas_call(
+        kernel,
+        out_shape=tuple(f32(shape) for shape in outs),
+        in_specs=[pl.BlockSpec(memory_space=pltpu.VMEM)] * len(args),
+        out_specs=tuple(pl.BlockSpec(memory_space=pltpu.VMEM) for _ in outs),
+        scratch_shapes=[pltpu.VMEM(shape, jnp.float32) for shape in scratch],
+        compiler_params=pltpu.CompilerParams(vmem_limit_bytes=VMEM_LIMIT),
+    )(*args)
+
+
+def swapped(value, axis, first):
+    count = lax.axis_size(axis)
+    pairs = [(i, i + 1) for i in range(first, count - 1, 2)]
+    if not pairs:
+        return jnp.zeros_like(value)
+    return lax.ppermute(value, axis, pairs + [(j, i) for i, j in pairs])
+
+
+def paired_shards(density, fixed_mask, load_mask, load_values):
+    planes, rows, lanes = density.shape
+    devices = 1
+    for axis in AXES:
+        devices *= lax.axis_size(axis)
+    grid = (rows * lax.axis_size("gy"), lanes * lax.axis_size("gz"))
+    count = 2 * planes
+    wide, tall = rows + 2 * FACE, rows + FACE
+    face = (5 * planes, FACE, lanes)
+    strips = (wide + 2 * tall, lanes)
+    row = (devices, 1, lanes)
+    fields, send_a, send_b = call(
+        pack_kernel, ((5 * planes, rows, lanes), face, face), density, fixed_mask, load_mask, load_values
+    )
+    density_own, node_own, own, send_a, send_b = call(
+        strip_kernel,
+        ((planes, wide, lanes), (4 * planes, tall, lanes), strips, strips, strips),
+        fields, swapped(send_a, "gy", 0), swapped(send_b, "gy", 1),
+    )
+    density_other = swapped(density_own, "gx", 0)
+    node_other = swapped(node_own, "gx", 0)
+    strip_own = own + swapped(send_a, "gz", 0) + swapped(send_b, "gz", 1)
+    strip_other = swapped(strip_own, "gx", 0)
+    window, first, strip_v, strip_g, dots = call(
+        functools.partial(filter_kernel, grid),
+        ((count, wide, lanes), (count, wide, lanes), (wide, lanes), (wide, lanes), row),
+        density_own, density_other, strip_own, strip_other,
+    )
+    dots = lax.all_to_all(dots, AXES, 0, 0, tiled=True)
+    table = element_table()
+    diagonal = float(table[0, 0, 0, 0])
+    plane = (tall, lanes)
+    filtered, basis, scale, dots = call(
+        functools.partial(solve_wrapped, grid, diagonal),
+        ((planes, rows, lanes), (5, 3, planes, rows, lanes), (planes, rows, lanes), row),
+        window, first, strip_v, strip_g, dots, node_own, node_other, strip_own, strip_other,
+        scratch=(
+            (5, 3, count) + plane,
+            (count,) + plane, (count,) + plane, (count,) + plane,
+            (6, count + 1, tall + 8, lanes), (12,) + plane, (12,) + plane, (6,) + plane, (6, tall + 8, lanes),
+            (1,) + plane, plane, plane, (3,) + plane, (4, 3, tall + 8, lanes), (6,) + plane, (6, tall + 8, lanes),
+            (4, 3) + plane,
+        ),
+    )
+    dots = lax.all_to_all(dots, AXES, 0, 0, tiled=True)
+    displacement, residual = call(combine_kernel, (load_values.shape, load_values.shape), dots, basis, scale)
+    return (filtered, displacement, residual)
+
+
+def solve_wrapped(
+    grid, diagonal, window, first, strip_v, strip_g, filter_dots, node_own, node_other, strip_own, strip_other,
+    filtered, fields, scale, dots, basis, modulus, inverse, free, pairs, kept, carried, near, far, *strip_scratch,
+):
+    solve_kernel(
+        grid, diagonal, window, first, strip_v, strip_g, filter_dots, node_own, node_other, strip_own, strip_other,
+        filtered, basis, scale, dots,
+        modulus, inverse, free, fields, pairs, kept, carried, near, far, *strip_scratch,
+    )
+
+
+def shards(density, fixed_mask, load_mask, load_values):
+    planes, rows, lanes = density.shape
+    if lax.axis_size("gx") == 2 and 2 * planes * SW == lanes and lanes == 128 and rows % 8 == 0:
+        return paired_shards(density, fixed_mask, load_mask, load_values)
+    return general_shards(density, fixed_mask, load_mask, load_values)
 
 
 def solution(mesh):

time: 1060 us -> 83 us (0.08); the launches traced: 1040 us -> 82.7 us
  local copies, waits for them, and re-layouts: 394 us -> 3.7 us
  blocking collectives: 406 us -> 26.7 us
  starting transfers between devices: 102 us -> 7.05 us
  other arithmetic: 76.1 us -> 0.02 us
  waiting for transfers between devices: 50.6 us -> 12.8 us
  Pallas kernels: 0 us -> 31.8 us
  between operations: 15.6 us -> 0.69 us
    psum x10 -> x0, blocking collectives: 406 us -> none  [the longest x6 245 us: residual_dot(): return lax.psum(jnp.sum(first * second), ('gx', 'gy', 'gz'))]
    mul x238 -> x0, local copies, waits for them, and re-layouts: 374 us -> none  [apply_stiffness(): stiffness[corner_a, corner_b, :, comp][:, None, None, None]]
    ppermute x39 -> x7, starting transfers between devices: 102 us -> 7.05 us  [swapped(): return lax.ppermute(value, axis, pairs + [(j, i) for i, j in pairs])]
    reduce_sum x10 -> x0, other arithmetic: 52.7 us -> none  [the longest x6 49.9 us: curvature_dot(): return lax.psum(jnp.sum(first * second), ('gx', 'gy', 'gz'))]
    ppermute x39 -> x7, waiting for transfers between devices: 50.6 us -> 12.8 us  [swapped(): return lax.ppermute(value, axis, pairs + [(j, i) for i, j in pairs])]
    pallas_call x0 -> x5, Pallas kernels: none -> 31.8 us  [call(): pl.pallas_call(kernel, out_shape=tuple((f32(shape) for shape in outs)), i...]
    all_to_all x0 -> x2, blocking collectives: none -> 26.7 us  [paired_shards(): dots = lax.all_to_all(dots, AXES, 0, 0, tiled=True)]
  transfers between devices with their start and end apart: 39 -> 7, of which waited for: 22 -> 4; matrix products, arithmetic and copies ran while one was open for 2% -> 0% of each run, Pallas kernels for 0% -> 2%
where the time goes in v1:
time: 83 us; the launch traced here: 82.7 us
  Pallas kernels  31.8 us (38%)
  blocking collectives  26.7 us (32%)
  waiting for transfers between devices  12.8 us (15%)
  starting transfers between devices  7.05 us (8%)
  local copies, waits for them, and re-layouts  3.7 us (4%)
    pallas_call x5, Pallas kernels, call(): pl.pallas_call(kernel, out_shape=tuple((f32(shape) for shape in outs)), i...  31.8 us
    all_to_all x2, blocking collectives, paired_shards(): dots = lax.all_to_all(dots, AXES, 0, 0, tiled=True)  26.7 us
    ppermute x7, waiting for transfers between devices, swapped(): return lax.ppermute(value, axis, pairs + [(j, i) for i, j in pairs])  12.8 us
    ppermute x7, starting transfers between devices, swapped(): return lax.ppermute(value, axis, pairs + [(j, i) for i, j in pairs])  7.05 us
    unnamed x8, local copies, waits for them, and re-layouts  3.7 us
  transfers between devices with their start and end apart: 7, of which 4 were waited for; matrix products, arithmetic and copies ran while one was open for 0% of the time, Pallas kernels for 2%

profile of v1, /device:TPU:0, one launch (start us, length us, event | category | flops | bytes accessed | tf_op | source)
XLA Modules:
  0.0 82.7 jit_solution(4224443636597357644)
XLA Ops:
  0.6 0.0 copy-start
  0.6 1.0 %copy-done = f32[3,4,64,128]{3,2,1,0:T(8,128)S(1)} copy-done((f32[3,4,64,128]{3,2,1,0:T(8,128)S(1)}, f32[3,4,64,128]{3,2,1,0:T(8,128)}, u32[]{:S(2)}) %copy-start) | copy-done | bytes 393240
  1.6 0.0 copy-start.1
  1.6 0.9 %copy-done.1 = f32[4,64,128]{2,1,0:T(8,128)S(1)} copy-done((f32[4,64,128]{2,1,0:T(8,128)S(1)}, f32[4,64,128]{2,1,0:T(8,128)}, u32[]{:S(2)}) %copy-start.1) | copy-done | bytes 131096
  2.5 0.0 copy-start.2
  2.5 0.9 %copy-done.2 = s32[4,64,128]{2,1,0:T(8,128)S(1)} copy-done((s32[4,64,128]{2,1,0:T(8,128)S(1)}, s32[4,64,128]{2,1,0:T(8,128)}, u32[]{:S(2)}) %copy-start.2) | copy-done | bytes 131096
  3.4 0.0 copy-start.3
  3.4 0.9 %copy-done.3 = s32[4,64,128]{2,1,0:T(8,128)S(1)} copy-done((s32[4,64,128]{2,1,0:T(8,128)S(1)}, s32[4,64,128]{2,1,0:T(8,128)}, u32[]{:S(2)}) %copy-start.3) | copy-done | bytes 131096
  4.3 0.1 shard_map.67
  4.4 0.5 collective-permute-start
  4.9 0.7 collective-permute-start.1
  5.6 0.3 collective-permute-done.from_a
  5.9 0.0 collective-permute-done.1.from_b
  5.9 0.5 shard_map.68
  6.3 2.9 %collective-permute-start.6 = (f32[16,72,128]{2,1,0:T(8,128)S(1)}, f32[16,72,128]{2,1,0:T(8,128)S(1)}, u32[]{:S(2)}, u32[]{:S(2)}) collective-permute-start(f32[16,72,128]{2,1,0:T(8,128)S(1)} %get-tuple-element.34.node_own), channel_id=1, source_target_pairs={{0,16},{16,0},{1,17},{17,1},{2,18},{18,2},{3,19},{19,3},{4,20},{20... | collective-permute-start | bytes 1769480 | tf_op jit(solution)/shard_map/ppermute | solution.py:808
  9.3 1.6 %collective-permute-start.3 = (f32[224,128]{1,0:T(8,128)S(1)}, f32[224,128]{1,0:T(8,128)S(1)}, u32[]{:S(2)}, u32[]{:S(2)}) collective-permute-start(f32[224,128]{1,0:T(8,128)S(1)} %get-tuple-element.27), channel_id=1, source_target_pairs={{0,1},{2,3},{1,0},{3,2},{4,5},{6,7},{5,4},{7,6},{8,9},{10,11},{9,8... | collective-permute-start | bytes 344072 | tf_op jit(solution)/shard_map/ppermute | solution.py:808
  10.8 0.7 collective-permute-start.4
  11.5 0.6 collective-permute-start.2
  12.1 2.0 %collective-permute-done.3 = f32[224,128]{1,0:T(8,128)S(1)} collective-permute-done((f32[224,128]{1,0:T(8,128)S(1)}, f32[224,128]{1,0:T(8,128)S(1)}, u32[]{:S(2)}, u32[]{:S(2)}) %collective-permute-start.3) | collective-permute-done | bytes 114720 | tf_op jit(solution)/shard_map/ppermute | solution.py:808
  14.1 0.0 collective-permute-done.4
  14.1 0.1 collective-permute-start.5
  14.2 8.1 %collective-permute-done.2.other = f32[4,80,128]{2,1,0:T(8,128)S(1)} collective-permute-done((f32[4,80,128]{2,1,0:T(8,128)S(1)}, f32[4,80,128]{2,1,0:T(8,128)S(1)}, u32[]{:S(2)}, u32[]{:S(2)}) %collective-permute-start.2) | collective-permute-done | bytes 163872 | tf_op jit(solution)/shard_map/ppermute | solution.py:808
  22.3 2.5 %collective-permute-done.5.strip_other = f32[224,128]{1,0:T(8,128)S(1)} collective-permute-done((f32[224,128]{1,0:T(8,128)S(1)}, f32[224,128]{1,0:T(8,128)S(1)}, u32[]{:S(2)}, u32[]{:S(2)}) %collective-permute-start.5) | collective-permute-done | bytes 114720 | tf_op jit(solution)/shard_map/ppermute | solution.py:808
  24.8 1.9 %shard_map.69 = (f32[8,80,128]{2,1,0:T(8,128)S(1)}, f32[8,80,128]{2,1,0:T(8,128)S(1)}, f32[80,128]{1,0:T(8,128)S(1)}, f32[80,128]{1,0:T(8,128)S(1)}, f32[32,1,128]{2,1,0:T(1,128)S(1)}) custom-call(f32[4,80,128]{2,1,0:T(8,128)S(1)} %get-tuple-element.25.own, f32[4,80,128]{2,1,0:T(8,128)S(1)} %collective-permute-done.2.other, ...), custom_call_target="tpu_custom_call" | custom-call | tf_op jit(solution)/shard_map/pallas_call | solution.py:793
  26.7 17.2 %all_to_all.10.filter_dots = f32[32,1,128]{2,1,0:T(1,128)S(1)} all-to-all(f32[32,1,128]{2,1,0:T(1,128)S(1)} %get-tuple-element.33), channel_id=1, replica_groups=mesh['gx'=2,'gy'=4,'gz'=4] {'gx','gy','gz'}, dimensions={0} | all-to-all | bytes 32768 | tf_op jit(solution)/shard_map/all_to_all | solution.py:839
  43.8 0.0 collective-permute-done.6.node_other
  43.8 28.1 %shard_map.70 = (f32[4,64,128]{2,1,0:T(8,128)}, f32[5,3,4,64,128]{4,3,2,1,0:T(8,128)S(1)}, f32[4,64,128]{2,1,0:T(8,128)S(1)}, f32[32,1,128]{2,1,0:T(1,128)S(1)}) custom-call(f32[8,80,128]{2,1,0:T(8,128)S(1)} %get-tuple-element.29.window, f32[8,80,128]{2,1,0:T(8,128)S(1)} %get-tuple-element.30.first, f32[80,128]{1,0:T(8,128)S(1)} %get-tuple-element.31.strip_v, ...), custom_call_target="tpu_custom_call" | custom-call | tf_op jit(solution)/shard_map/pallas_call | solution.py:793
  71.9 9.5 %all_to_all.11.dots = f32[32,1,128]{2,1,0:T(1,128)S(1)} all-to-all(f32[32,1,128]{2,1,0:T(1,128)S(1)} %get-tuple-element.36), channel_id=1, replica_groups=mesh['gx'=2,'gy'=4,'gz'=4] {'gx','gy','gz'}, dimensions={0} | all-to-all | bytes 32768 | tf_op jit(solution)/shard_map/all_to_all | solution.py:855
  81.4 1.3 %shard_map.71 = (f32[3,4,64,128]{3,2,1,0:T(8,128)}, f32[3,4,64,128]{3,2,1,0:T(8,128)}) custom-call(f32[32,1,128]{2,1,0:T(1,128)S(1)} %all_to_all.11.dots, f32[5,3,4,64,128]{4,3,2,1,0:T(8,128)S(1)} %get-tuple-element.37.basis, f32[4,64,128]{2,1,0:T(8,128)S(1)} %get-tuple-element.38.scale), custom_call_target="tpu_custom_call" | custom-call | tf_op jit(solution)/shard_map/pallas_call | solution.py:793
  (1 shorter events, 0.0 us)
Async XLA Ops:
  0.6 1.0 %copy-start = (f32[3,4,64,128]{3,2,1,0:T(8,128)S(1)}, f32[3,4,64,128]{3,2,1,0:T(8,128)}, u32[]{:S(2)}) copy-start(f32[3,4,64,128]{3,2,1,0:T(8,128)} %load_values.1) | copy-start | bytes 1179652
  1.6 0.9 %copy-start.1 = (f32[4,64,128]{2,1,0:T(8,128)S(1)}, f32[4,64,128]{2,1,0:T(8,128)}, u32[]{:S(2)}) copy-start(f32[4,64,128]{2,1,0:T(8,128)} %density.1) | copy-start | bytes 393220
  2.5 0.9 %copy-start.2 = (s32[4,64,128]{2,1,0:T(8,128)S(1)}, s32[4,64,128]{2,1,0:T(8,128)}, u32[]{:S(2)}) copy-start(s32[4,64,128]{2,1,0:T(8,128)} %fixed.1) | copy-start | bytes 393220
  3.4 0.9 %copy-start.3 = (s32[4,64,128]{2,1,0:T(8,128)S(1)}, s32[4,64,128]{2,1,0:T(8,128)}, u32[]{:S(2)}) copy-start(s32[4,64,128]{2,1,0:T(8,128)} %load_mask.1) | copy-start | bytes 393220
  4.4 1.4 %collective-permute-start = (f32[20,8,128]{2,1,0:T(8,128)S(1)}, f32[20,8,128]{2,1,0:T(8,128)S(1)}, u32[]{:S(2)}, u32[]{:S(2)}) collective-permute-start(f32[20,8,128]{2,1,0:T(8,128)S(1)} %get-tuple-element.23), channel_id=1, source_target_pairs={{0,4},{8,12},{4,0},{12,8},{1,5},{9,13},{5,1},{13,9},{2,6},{10,14},... | collective-permute-start | bytes 245768 | tf_op jit(solution)/shard_map/ppermute | solution.py:808
  4.9 0.9 %collective-permute-start.1 = (f32[20,8,128]{2,1,0:T(8,128)S(1)}, f32[20,8,128]{2,1,0:T(8,128)S(1)}, u32[]{:S(2)}, u32[]{:S(2)}) collective-permute-start(f32[20,8,128]{2,1,0:T(8,128)S(1)} %get-tuple-element.24), channel_id=1, source_target_pairs={{4,8},{8,4},{5,9},{9,5},{6,10},{10,6},{7,11},{11,7},{20,24},{24,20... | collective-permute-start | bytes 245768 | tf_op jit(solution)/shard_map/ppermute | solution.py:808
  6.3 37.5 %collective-permute-start.6 = (f32[16,72,128]{2,1,0:T(8,128)S(1)}, f32[16,72,128]{2,1,0:T(8,128)S(1)}, u32[]{:S(2)}, u32[]{:S(2)}) collective-permute-start(f32[16,72,128]{2,1,0:T(8,128)S(1)} %get-tuple-element.34.node_own), channel_id=1, source_target_pairs={{0,16},{16,0},{1,17},{17,1},{2,18},{18,2},{3,19},{19,3},{4,20},{20... | collective-permute-start | bytes 1769480 | tf_op jit(solution)/shard_map/ppermute | solution.py:808
  9.3 4.8 %collective-permute-start.3 = (f32[224,128]{1,0:T(8,128)S(1)}, f32[224,128]{1,0:T(8,128)S(1)}, u32[]{:S(2)}, u32[]{:S(2)}) collective-permute-start(f32[224,128]{1,0:T(8,128)S(1)} %get-tuple-element.27), channel_id=1, source_target_pairs={{0,1},{2,3},{1,0},{3,2},{4,5},{6,7},{5,4},{7,6},{8,9},{10,11},{9,8... | collective-permute-start | bytes 344072 | tf_op jit(solution)/shard_map/ppermute | solution.py:808
  10.8 3.2 %collective-permute-start.4 = (f32[224,128]{1,0:T(8,128)S(1)}, f32[224,128]{1,0:T(8,128)S(1)}, u32[]{:S(2)}, u32[]{:S(2)}) collective-permute-start(f32[224,128]{1,0:T(8,128)S(1)} %get-tuple-element.28), channel_id=1, source_target_pairs={{1,2},{2,1},{5,6},{6,5},{9,10},{10,9},{13,14},{14,13},{17,18},{18,... | collective-permute-start | bytes 344072 | tf_op jit(solution)/shard_map/ppermute | solution.py:808
  11.5 10.8 %collective-permute-start.2 = (f32[4,80,128]{2,1,0:T(8,128)S(1)}, f32[4,80,128]{2,1,0:T(8,128)S(1)}, u32[]{:S(2)}, u32[]{:S(2)}) collective-permute-start(f32[4,80,128]{2,1,0:T(8,128)S(1)} %get-tuple-element.25.own), channel_id=1, source_target_pairs={{0,16},{16,0},{1,17},{17,1},{2,18},{18,2},{3,19},{19,3},{4,20},{20... | collective-permute-start | bytes 491528 | tf_op jit(solution)/shard_map/ppermute | solution.py:808
  14.1 10.7 %collective-permute-start.5 = (f32[224,128]{1,0:T(8,128)S(1)}, f32[224,128]{1,0:T(8,128)S(1)}, u32[]{:S(2)}, u32[]{:S(2)}) collective-permute-start(f32[224,128]{1,0:T(8,128)S(1)} %add_add_fusion.strip_own), channel_id=1, source_target_pairs={{0,16},{16,0},{1,17},{17,1},{2,18},{18,2},{3,19},{19,3},{4,20},{20... | collective-permute-start | bytes 344072 | tf_op jit(solution)/shard_map/ppermute | solution.py:808

commit v2 on v1

--- a/solution.py
+++ b/solution.py
@@ -255,97 +255,87 @@
     return jnp.where(jnp.full(first.shape, flag, jnp.int32) == 0, first, second)
 
 
-def pack_kernel(density, fixed, load_mask, load_values, fields, send_a, send_b):
+def face_kernel(density, fixed, load_mask, load_values, send_a, send_b, bare_a, bare_b, d, f, m, v, done):
     planes, rows, _ = density.shape
+    copies = []
+    for side, at in ((0, 0), (1, rows - FACE)):
+        for source, target in ((density, d), (fixed, f), (load_mask, m)):
+            copies.append((source.at[:, at : at + FACE, :], target.at[side]))
+        copies.append((load_values.at[:, :, at : at + FACE, :], v.at[side]))
+    copies = [pltpu.make_async_copy(src, dst, done.at[n]) for n, (src, dst) in enumerate(copies)]
+    for copy in copies:
+        copy.start()
+    for copy in copies:
+        copy.wait()
     odd = lax.rem(lax.axis_index("gy"), 2)
+    for send, bare, side in ((send_a, bare_a, 1 - odd), (send_b, bare_b, odd)):
+        free = (1 - f[side]).astype(jnp.float32)
+        loaded = free * m[side].astype(jnp.float32)
+        send[:planes] = d[side]
+        bare[...] = d[side]
+        send[planes : 2 * planes] = free
+        for c in range(3):
+            send[(2 + c) * planes : (3 + c) * planes] = loaded * v[side, c]
+
+
+def strip_kernel(
+    density, other, fixed, load_mask, load_values, from_a, from_b, bare_a, bare_b, window, nodes, strips
+):
+    planes, rows, lanes = density.shape
+    wide, tall = rows + 2 * FACE, rows + FACE
+    mine = lax.axis_index("gx") * planes
+    odd_y = lax.rem(lax.axis_index("gy"), 2)
+    row = rows_of((FACE, lanes))
+    for source, a, b, at in ((density, from_a, from_b, mine), (other, bare_a, bare_b, planes - mine)):
+        for p in range(planes):
+            window[at + p, :rows] = source[p]
+            window[at + p, rows : rows + FACE] = either(odd_y, a[p], b[p])
+            window[at + p, rows + FACE :] = either(odd_y, b[p], a[p])
+    lane = lanes_of((wide, lanes))
+    packed = jnp.zeros((wide, lanes), jnp.float32)
+    for p in range(2 * planes):
+        packed = jnp.where(lane // SW == p, turned(window[p], SW * p + 8, 1), packed)
+    strips[:wide] = packed
     for p in range(planes):
         free = (1 - fixed[p]).astype(jnp.float32)
         loaded = free * load_mask[p].astype(jnp.float32)
-        fields[p] = density[p]
-        fields[planes + p] = free
+        nodes[p, :rows] = free
         for c in range(3):
-            fields[(2 + c) * planes + p] = loaded * load_values[c, p]
-    row_a = pl.multiple_of((1 - odd) * (rows - FACE), FACE)
-    row_b = pl.multiple_of(odd * (rows - FACE), FACE)
-    send_a[...] = fields[:, pl.ds(row_a, FACE), :]
-    send_b[...] = fields[:, pl.ds(row_b, FACE), :]
-
-
-def strip_kernel(fields, from_a, from_b, density_out, node_out, own, send_a, send_b):
-    total, rows, lanes = fields.shape
-    planes = total // 5
-    odd_y = lax.rem(lax.axis_index("gy"), 2)
-    odd_z = lax.rem(lax.axis_index("gz"), 2)
-    row = rows_of((FACE, lanes))
-    for q in range(total):
-        above = either(odd_y, from_a[q], from_b[q])
-        below = either(odd_y, from_b[q], from_a[q])
-        if q < planes:
-            density_out[q, :rows] = fields[q]
-            density_out[q, rows : rows + FACE] = above
-            density_out[q, rows + FACE :] = below
-        else:
-            node_out[q - planes, :rows] = fields[q]
-            node_out[q - planes, rows:] = jnp.where(row < HALO, above, below)
-    wide = rows + 2 * FACE
-    tall = rows + FACE
-    own[:wide] = jnp.zeros((wide, lanes), jnp.float32)
-    lane = lanes_of((wide, lanes))
-    low = jnp.zeros((wide, lanes), jnp.float32)
-    high = low
-    for p in range(planes):
-        value = density_out[p]
-        base = SW * p
-        low = jnp.where((lane >= base) & (lane < base + 8), turned(value, base, 1), low)
-        high = jnp.where((lane >= base + 8) & (lane < base + 16), turned(value, base + 16, 1), high)
-    send_a[:wide] = either(odd_z, high, low)
-    send_b[:wide] = either(odd_z, low, high)
+            nodes[(1 + c) * planes + p, :rows] = loaded * load_values[c, p]
+    for q in range(4 * planes):
+        above = either(odd_y, from_a[planes + q], from_b[planes + q])
+        below = either(odd_y, from_b[planes + q], from_a[planes + q])
+        nodes[q, rows:] = jnp.where(row < HALO, above, below)
     lane = lanes_of((tall, lanes))
     for pair in range(2):
-        low = jnp.zeros((tall, lanes), jnp.float32)
-        high = low
-        mine = low
-        for half in range(2):
-            for p in range(planes):
-                value = node_out[(2 * pair + half) * planes + p]
-                base = SW * p + (lanes // 2) * half
-                four = turned(value, base + 4, 1)
-                twelve = turned(value, base + 12, 1)
-                part = (lane - base) // 4
-                inside = (lane >= base) & (lane < base + SW)
-                mine = jnp.where(inside & (part == 0), four, mine)
-                low = jnp.where(inside & (part == 1), four, low)
-                high = jnp.where(inside & (part == 2), twelve, high)
-                mine = jnp.where(inside & (part == 3), twelve, mine)
-        at = wide + pair * tall
-        own[at : at + tall] = mine
-        send_a[at : at + tall] = either(odd_z, high, low)
-        send_b[at : at + tall] = either(odd_z, low, high)
-
-
-def filter_kernel(grid, own, other, strip_own, strip_other, window, first, strip_v, strip_g, dots):
-    planes, wide, lanes = own.shape
+        packed = jnp.zeros((tall, lanes), jnp.float32)
+        for q in range(2 * planes):
+            value = nodes[2 * planes * pair + q]
+            packed = jnp.where(lane // SW == q, turned(value, SW * q + 12, 1), packed)
+        strips[wide + pair * tall : wide + (pair + 1) * tall] = packed
+
+
+def filter_kernel(grid, window, strips, from_a, from_b, first, strip_v, strip_g, node_strips, dots):
+    count, wide, lanes = window.shape
     rows = wide - 2 * FACE
-    count = 2 * planes
+    planes = count // 2
     total_y, total_z = grid
-    gx = lax.axis_index("gx")
+    mine = lax.axis_index("gx") * planes
+    odd_z = lax.rem(lax.axis_index("gz"), 2)
     base_y = lax.axis_index("gy") * rows
     base_z = lax.axis_index("gz") * lanes
-    mine = gx * planes
-    window[pl.ds(mine, planes)] = own[...]
-    window[pl.ds(planes - mine, planes)] = other[...]
     shape = (wide, lanes)
     lane = lanes_of(shape)
     row = rows_of(shape)
-    lower = either(gx, strip_own[:wide], strip_other[:wide])
-    upper = either(gx, strip_other[:wide], strip_own[:wide])
-    strip_v[...] = jnp.where(lane < lanes // 2, lower, turned(upper, lanes // 2, 1))
+    place = lax.rem(lane, SW)
+    strip_v[...] = jnp.where(
+        place < 8, either(odd_z, from_b[:wide], from_a[:wide]), either(odd_z, from_a[:wide], from_b[:wide])
+    )
     at_y = base_y + jnp.where(row < rows + FACE, row, row - wide)
     pass_y = ((at_y >= 0) & (at_y < total_y - 1)).astype(jnp.float32)
     pass_z = (base_z + lane < total_z - 1).astype(jnp.float32)
     back_z = (base_z + lane > 0).astype(jnp.float32)
-    place = lax.rem(lane, SW)
-    at_strip = base_z + jnp.where(place < 8, lanes + place, place - SW)
+    at_strip = base_z + jnp.where(place < 8, place - 8, lanes - 8 + place)
     strip_pass = ((at_strip >= 0) & (at_strip < total_z - 1)).astype(jnp.float32)
     strip_back = ((at_strip >= 1) & (at_strip < total_z)).astype(jnp.float32)
 
@@ -358,8 +348,8 @@
         result = (value - source[jnp.minimum(p + 1, count - 1)]) + (value - source[jnp.maximum(p - 1, 0)])
         result = result + along_y(value)
         side = strip[...]
-        ahead = jnp.where(lane == lanes - 1, turned(side, lanes - 1 - SW * p, 1), turned(value, -1, 1))
-        behind = jnp.where(lane == 0, turned(side, 0 - (SW * p + SW - 1), 1), turned(value, 1, 1))
+        ahead = jnp.where(lane == lanes - 1, turned(side, lanes - 1 - (SW * p + 8), 1), turned(value, -1, 1))
+        behind = jnp.where(lane == 0, turned(side, 0 - (SW * p + 7), 1), turned(value, 1, 1))
         result = result + (value - ahead) * pass_z + (value - behind) * back_z
         return filter_weight * result
 
@@ -372,10 +362,10 @@
     edge_low = jnp.zeros(shape, jnp.float32)
     edge_high = edge_low
     for p in range(count):
-        edge_low = jnp.where(lane == SW * p + SW - 1, turned(window[p], SW * p + SW - 1, 1), edge_low)
-        edge_high = jnp.where(lane == SW * p, turned(window[p], SW * p - (lanes - 1), 1), edge_high)
-    ahead = jnp.where(place == SW - 1, edge_low, turned(value, -1, 1))
-    behind = jnp.where(place == 0, edge_high, turned(value, 1, 1))
+        edge_low = jnp.where(lane == SW * p + 7, turned(window[p], SW * p + 7, 1), edge_low)
+        edge_high = jnp.where(lane == SW * p + 8, turned(window[p], SW * p + 8 - (lanes - 1), 1), edge_high)
+    ahead = jnp.where(place == 7, edge_low, turned(value, -1, 1))
+    behind = jnp.where(place == 8, edge_high, turned(value, 1, 1))
     result = along_y(value) + (value - ahead) * strip_pass + (value - behind) * strip_back
     ahead = jnp.where(lane < lanes - SW, turned(value, -SW, 1) - value, 0.0)
     result = result + turned(ahead, SW, 1) - ahead
@@ -393,6 +383,10 @@
 
     zero = jnp.zeros((8, lanes), jnp.float32)
     spread(lax.fori_loop(0, planes, add_dots, (zero,) * 4), dots)
+    half = node_strips.shape[0] // 2
+    place = lax.rem(lanes_of((half, lanes)), SW)
+    node_strips[:half] = jnp.where(place < 12, strips[wide:], either(odd_z, from_a[wide:], from_b[wide:]))
+    node_strips[half:] = either(odd_z, from_b[wide:], from_a[wide:])
 
 
 def spread(sums, dots):
@@ -451,9 +445,9 @@
 
 def solve_kernel(
     grid, diagonal, window, first, strip_v, strip_g, filter_dots, node_own, node_other, strip_own, strip_other,
-    filtered, basis, scale, dots,
-    modulus, inverse, free, fields, pairs, kept, carried, near, far,
-    s_modulus, s_inverse, s_free, s_old, s_disp, s_near, s_far, s_edge,
+    filtered, fields, strip_fields, scale, strip_scale, dots,
+    basis, modulus, inverse, free, pairs, kept, carried, near, far,
+    s_basis, s_modulus, s_inverse, s_free, s_pairs, s_near, s_far, s_part, s_disp,
 ):
     count, wide, lanes = window.shape
     rows = wide - 2 * FACE
@@ -482,7 +476,7 @@
     at_y = base_y + jnp.where(row < rows + FACE, row, row - wide)
     inside_y = (at_y >= 0) & (at_y < total_y)
     place = lax.rem(lane, SW)
-    at_strip = base_z + jnp.where(place < 8, lanes + place, place - SW)
+    at_strip = base_z + jnp.where(place < 8, place - 8, lanes - 8 + place)
     inside_strip = inside_y & (at_strip >= 0) & (at_strip < total_z)
     small = rows_of((8, lanes))
 
@@ -490,133 +484,144 @@
         tail = jnp.where(small < HALO, value[rows : rows + 8], value[rows + 8 :])
         return value[:rows], tail
 
-    def put(ref, index, value):
-        head, tail = folded(value)
-        ref[index, :rows] = head
-        ref[index, rows:] = tail
-
     def moduli_of(v, g):
         value = weight_v * v + weight_g * g
-        return value, MIN_MODULUS + (1.0 - MIN_MODULUS) * value * value * jnp.abs(value)
-
-    side = moduli_of(strip_v[...], strip_g[...])[1]
-    side = jnp.where(inside_strip, side, 0.0)
+        return MIN_MODULUS + (1.0 - MIN_MODULUS) * value * value * jnp.abs(value)
 
     def inverted(total, open_nodes):
         return jnp.where(total > 0.0, open_nodes / jnp.where(total > 0.0, diagonal * total, 1.0), 0.0)
 
-    node_at = [pl.ds(pl.multiple_of(mine, planes), planes), pl.ds(pl.multiple_of(planes - mine, planes), planes)]
-    for f in range(4):
-        for source, at in zip((node_own, node_other), node_at):
-            value = source[f * planes : (f + 1) * planes]
-            if f == 0:
-                free[at] = value
-            else:
-                basis[0, f - 1, at] = value
-
-    s_line = jnp.zeros(shape, jnp.float32)
-    previous = jnp.zeros(shape, jnp.float32)
-    for p in range(count):
-        value, mod = moduli_of(window[p], first[p])
-        mod = jnp.where(inside_y, mod, 0.0)
-        put(modulus, p, mod)
-        edge = turned(side, 0 - (SW * p + SW - 1), 1)
-        across = mod + jnp.where(lane == 0, edge, turned(mod, 1, 1))
-        across = across + turned(across, 1, 0)
-        head, tail = folded(across + previous)
-        previous = across
-        inverse[p, :rows] = inverted(head, free[p, :rows])
-        inverse[p, rows:] = inverted(tail, free[p, rows:])
-        s_line = jnp.where((lane >= SW * p) & (lane < SW * p + 4), turned(mod, SW * p + 4, 1), s_line)
-        s_line = jnp.where((lane >= SW * p + 12) & (lane < SW * p + 16), turned(mod, SW * p + 12, 1), s_line)
-    for p in range(planes):
-        v = window[mine + p]
-        g = first[mine + p]
-        filtered[p] = (weight_v * v + weight_g * g)[:rows]
-
-    s_mod = jnp.where(
-        (place >= 4) & (place < 8), turned(side, 4, 1), jnp.where((place >= 8) & (place < 12), turned(side, -4, 1), s_line)
-    )
-    put(s_modulus, 0, s_mod)
-    across = s_mod + jnp.where(place == 8, turned(side, -3, 1), turned(s_mod, 1, 1))
-    across = across + turned(across, 1, 0)
-    across = across + jnp.where(lane < SW, 0.0, turned(across, SW, 1))
-    s_head, s_tail = folded(across)
-
+    tall_lane = lanes_of((tall, lanes))
+    for source, strip, at in ((node_own, strip_own, mine), (node_other, strip_other, planes - mine)):
+        for f in range(4):
+            for p in range(planes):
+                q = (f % 2) * planes + p
+                begin = (2 + f // 2) * tall
+                before = turned(strip[begin : begin + tall], lanes - HALO - (SW * q + 8), 1)
+                value = jnp.where(tall_lane < lanes - HALO, source[f * planes + p], before)
+                if f == 0:
+                    free[at + p] = value
+                else:
+                    basis[0, f - 1, at + p] = value
     half = lanes // 2
+    left = tall_lane < half
     for pair in range(2):
-        at = wide + pair * tall
+        at = pair * tall
         lower = either(gx, strip_own[at : at + tall], strip_other[at : at + tall])
         upper = either(gx, strip_other[at : at + tall], strip_own[at : at + tall])
-        left = lanes_of((tall, lanes)) < half
         one = jnp.where(left, lower, turned(upper, half, 1))
         two = jnp.where(left, turned(lower, half, 1), upper)
         for k, value in ((2 * pair, one), (2 * pair + 1, two)):
             if k == 0:
                 s_free[...] = value
             else:
-                s_old[k - 1] = value
-    s_inverse[:rows] = inverted(s_head, s_free[:rows])
-    s_inverse[rows:] = inverted(s_tail, s_free[rows:])
-    for c in range(3):
-        s_disp[0, c, :tall] = s_inverse[...] * s_old[c]
-        s_disp[0, c, tall : tall + 1] = s_disp[0, c, 0:1]
+                s_basis[0, k - 1] = value
+
+    side = jnp.where(inside_strip, moduli_of(strip_v[...], strip_g[...]), 0.0)
+    s_mod = turned(side, 4, 1)
+    s_back = jnp.zeros(shape, jnp.float32)
+    previous = jnp.zeros(shape, jnp.float32)
+    for p in range(count):
+        mod = jnp.where(inside_y, moduli_of(window[p], first[p]), 0.0)
+        before = turned(side, lanes - HALO - (SW * p + 4), 1)
+        across = jnp.where(lane >= lanes - HALO, before, mod)
+        head, tail = folded(across)
+        modulus[p, :rows] = head
+        modulus[p, rows:] = tail
+        across = across + turned(jnp.where(lane >= lanes - HALO - 1, before, mod), 1, 1)
+        across = across + turned(across, 1, 0)
+        head, tail = folded(across + previous)
+        previous = across
+        inverse[p, :rows] = inverted(head, free[p, :rows])
+        inverse[p, rows:] = inverted(tail, free[p, rows:])
+        inside = (lane // SW == p) & (place < 12)
+        s_mod = jnp.where(inside, turned(mod, SW * p + 12, 1), s_mod)
+        s_back = jnp.where(inside, turned(mod, SW * p + 13, 1), s_back)
+    for p in range(planes):
+        filtered[p] = (weight_v * window[mine + p] + weight_g * first[mine + p])[:rows]
+    head, tail = folded(s_mod)
+    s_modulus[:rows] = head
+    s_modulus[rows:] = tail
+    across = s_mod + jnp.where(place < 12, s_back, turned(s_mod, 1, 1))
+    across = across + turned(across, 1, 0)
+    across = across + jnp.where(lane < SW, 0.0, turned(across, SW, 1))
+    head, tail = folded(across)
+    s_inverse[:rows] = inverted(head, s_free[:rows])
+    s_inverse[rows:] = inverted(tail, s_free[rows:])
 
     lane = lanes_of((8, lanes))
     last_plane = lane >= lanes - SW
     first_plane = lane < SW
-
+    starts = range(0, tall, 8)
+
+    def strip_pairs():
+        for c in range(3):
+            for r in starts:
+                value = s_disp[c, r : r + 8]
+                ahead = turned(value, -1, 1)
+                s_part[2 * c, r : r + 8] = value + ahead
+                s_part[2 * c + 1, r : r + 8] = ahead - value
+        for k in range(6):
+            for r in starts:
+                value = s_part[k, r : r + 8]
+                beside = jnp.where(last_plane, 0.0, turned(value, -SW, 1))
+                s_pairs[2 * k, r : r + 8] = value + beside
+                s_pairs[2 * k + 1, r : r + 8] = beside - value
+            for n in (2 * k, 2 * k + 1):
+                s_pairs[n, tall : tall + 1] = s_pairs[n, 0:1]
+
+    for c in range(3):
+        s_disp[c] = s_inverse[...] * s_basis[0, c]
+    strip_pairs()
     for j in range(4):
-        for t in range(tiles):
-            r = 8 * t
+        for r in starts:
             u = []
             for c in range(3):
-                now = s_disp[j, c, r : r + 8]
-                after = s_disp[j, c, r + 1 : r + 9]
                 modes = {}
-                for beta_, value in ((0, now + after), (1, after - now)):
-                    beside = jnp.where(last_plane, 0.0, turned(value, -SW, 1))
-                    for alpha, across in ((0, value + beside), (1, beside - value)):
-                        next_z = turned(across, -1, 1)
-                        if (alpha, beta_) != (0, 0):
-                            modes[alpha, beta_, 0] = across + next_z
-                        modes[alpha, beta_, 1] = next_z - across
+                for g in range(2):
+                    for alpha in range(2):
+                        k = 2 * (2 * c + g) + alpha
+                        now = s_pairs[k, r : r + 8]
+                        after = s_pairs[k, r + 1 : r + 9]
+                        if (alpha, g) != (0, 0):
+                            modes[alpha, 0, g] = now + after
+                        modes[alpha, 1, g] = after - now
                 u.append(modes)
-            f = element_forces(u, s_modulus[0, r : r + 8])
+            f = element_forces(u, s_modulus[r : r + 8])
             for c in range(3):
                 for g in range(2):
-                    t_beta = []
-                    for beta_ in range(2):
-                        diff = f[c][1, beta_, g]
-                        if (beta_, g) == (0, 0):
-                            lower, upper = -diff, diff
+                    for alpha in range(2):
+                        k = 2 * (2 * c + g) + alpha
+                        diff = f[c][alpha, 1, g]
+                        if (alpha, g) == (0, 0):
+                            s_near[k, r : r + 8] = -diff
+                            s_far[k, r + 8 : r + 16] = diff
                         else:
-                            total = f[c][0, beta_, g]
-                            lower, upper = total - diff, total + diff
-                        t_beta.append(lower + jnp.where(first_plane, 0.0, turned(upper, SW, 1)))
-                    s_near[2 * c + g, r : r + 8] = t_beta[0] - t_beta[1]
-                    s_far[2 * c + g, r + 8 : r + 16] = t_beta[0] + t_beta[1]
+                            total = f[c][alpha, 0, g]
+                            s_near[k, r : r + 8] = total - diff
+                            s_far[k, r + 8 : r + 16] = total + diff
+        for k in range(12):
+            s_far[k, 7:8] = s_far[k, tall + 7 : tall + 8]
         for k in range(6):
-            s_far[k, 7:8] = s_far[k, tall + 7 : tall + 8]
-        for t in range(tiles):
-            r = 8 * t
-            for c in range(3):
-                total = s_near[2 * c, r : r + 8] + s_far[2 * c, r + 7 : r + 15]
-                diff = s_near[2 * c + 1, r : r + 8] + s_far[2 * c + 1, r + 7 : r + 15]
-                upper = total + diff
-                s_edge[j, c, r : r + 8] = upper
+            for r in starts:
+                total = s_near[2 * k, r : r + 8] + s_far[2 * k, r + 7 : r + 15]
+                diff = s_near[2 * k + 1, r : r + 8] + s_far[2 * k + 1, r + 7 : r + 15]
+                upper = jnp.where(first_plane, 0.0, turned(total + diff, SW, 1))
+                s_part[k, r : r + 8] = (total - diff) + upper
+        for c in range(3):
+            for r in starts:
+                total = s_part[2 * c, r : r + 8]
+                diff = s_part[2 * c + 1, r : r + 8]
+                out = (total - diff) + turned(total + diff, 1, 1)
+                new = s_free[r : r + 8] * out - SHIFTS[j] * s_basis[j, c, r : r + 8]
+                s_basis[j + 1, c, r : r + 8] = new
                 if j < 3:
-                    out = (total - diff) + turned(upper, 1, 1)
-                    new = s_free[r : r + 8] * out - SHIFTS[j] * s_old[c, r : r + 8]
-                    s_old[c, r : r + 8] = new
-                    s_disp[j + 1, c, r : r + 8] = s_inverse[r : r + 8] * new
+                    s_disp[c, r : r + 8] = s_inverse[r : r + 8] * new
         if j < 3:
-            for c in range(3):
-                s_disp[j + 1, c, tall : tall + 1] = s_disp[j + 1, c, 0:1]
-
-    def spread_z(j, c, p, r, disp):
-        edge = turned(s_disp[j, c, r : r + 8], lanes - 1 - (SW * p + 4), 1)
-        ahead = jnp.where(lane == lanes - 1, edge, turned(disp, -1, 1))
+            strip_pairs()
+
+    def spread_z(c, p, r, disp):
+        ahead = turned(disp, -1, 1)
         pairs[2 * c, p, r : r + 8] = disp + ahead
         pairs[2 * c + 1, p, r : r + 8] = ahead - disp
 
@@ -628,10 +633,9 @@
         pairs[k, count] = jnp.zeros(pairs.shape[2:], jnp.float32)
 
     def start_plane(p, carry):
-        for t in range(tiles):
-            r = 8 * t
+        for r in starts:
             for c in range(3):
-                spread_z(0, c, p, r, inverse[p, r : r + 8] * basis[0, c, p, r : r + 8])
+                spread_z(c, p, r, inverse[p, r : r + 8] * basis[0, c, p, r : r + 8])
         close_rows(p)
         return carry
 
@@ -648,16 +652,14 @@
     for j in range(4):
         low = gx * j
         high = count - 1 - j + gx * (j + 1)
-        for t in range(tiles):
-            r = 8 * t
+        for r in starts:
             for k, both in enumerate(along_rows(low, r)):
                 for beta_ in range(2):
                     kept[2 * k + beta_, r : r + 8] = both[beta_]
                     carried[2 * k + beta_, r : r + 8] = jnp.zeros((8, lanes), jnp.float32)
 
         def layer(p, state, j=j):
-            for t in range(tiles):
-                r = 8 * t
+            for r in starts:
                 upper_rows = along_rows(p + 1, r)
                 u = []
                 for c in range(3):
@@ -691,19 +693,17 @@
                         far[2 * c + g, r + 8 : r + 16] = t_beta[0] + t_beta[1]
             for k in range(6):
                 far[k, 7:8] = far[k, tall + 7 : tall + 8]
-            for t in range(tiles):
-                r = 8 * t
+            for r in starts:
                 open_nodes = free[p, r : r + 8]
                 inv = inverse[p, r : r + 8]
                 for c in range(3):
                     total = near[2 * c, r : r + 8] + far[2 * c, r + 7 : r + 15]
                     diff = near[2 * c + 1, r : r + 8] + far[2 * c + 1, r + 7 : r + 15]
-                    edge = turned(s_edge[j, c, r : r + 8], 0 - (SW * p + 11), 1)
-                    out = (total - diff) + jnp.where(lane == 0, edge, turned(total + diff, 1, 1))
+                    out = (total - diff) + turned(total + diff, 1, 1)
                     new = open_nodes * out - SHIFTS[j] * basis[j, c, p, r : r + 8]
                     basis[j + 1, c, p, r : r + 8] = new
                     if j < 3:
-                        spread_z(j + 1, c, p, r, inv * new)
+                        spread_z(c, p, r, inv * new)
             if j < 3:
                 close_rows(p)
             return state
@@ -711,12 +711,12 @@
         lax.fori_loop(low, high, layer, 0)
 
     order = [(i, k) for i in range(4) for k in range(i, 5)]
+    zero = jnp.zeros((8, lanes), jnp.float32)
 
     def add_dots(p, sums):
         plane = mine + p
         sums = list(sums)
-        for t in range(rows // 8):
-            r = 8 * t
+        for r in range(0, rows, 8):
             inv = inverse[plane, r : r + 8]
             scale[p, r : r + 8] = inv
             for c in range(3):
@@ -728,11 +728,27 @@
                     sums[n] = sums[n] + ws[i] * ys[k]
         return tuple(sums)
 
-    zero = jnp.zeros((8, lanes), jnp.float32)
-    spread(lax.fori_loop(0, planes, add_dots, (zero,) * len(order)), dots)
-
-
-def combine_kernel(dots, basis, scale, displacement, residual):
+    main = lax.fori_loop(0, planes, add_dots, (zero,) * len(order))
+    extra = [zero] * len(order)
+    for r in range(0, rows, 8):
+        inv = s_inverse[r : r + 8]
+        strip_scale[r : r + 8] = inv
+        for c in range(3):
+            ys = [s_basis[i, c, r : r + 8] for i in range(5)]
+            ws = [inv * y for y in ys[:4]]
+            for i in range(5):
+                strip_fields[i, c, r : r + 8] = ys[i]
+            for n, (i, k) in enumerate(order):
+                extra[n] = extra[n] + ws[i] * ys[k]
+    place = lax.rem(lane, SW)
+    own_lanes = (place >= 4) & (place < 12) & (lane // (SW * planes) == gx)
+    sums = [
+        jnp.where(lane < lanes - 8, value, 0.0) + jnp.where(own_lanes, more, 0.0) for value, more in zip(main, extra)
+    ]
+    spread(sums, dots)
+
+
+def combine_kernel(dots, basis, strips, scale, strip_scale, displacement, residual, ends):
     order = [(i, k) for i in range(4) for k in range(i, 5)]
     gram = {}
     for value, (i, k) in zip(gathered(dots, len(order)), order):
@@ -770,42 +786,56 @@
     disp = [jnp.broadcast_to(d, (8, lanes)) for d in disp]
     res = [jnp.broadcast_to(r, (8, lanes)) for r in res]
 
+    def combined(ys, inv):
+        first = disp[0] * ys[0]
+        second = res[0] * ys[0]
+        for i in range(1, 5):
+            second = second + res[i] * ys[i]
+            if i < 4:
+                first = first + disp[i] * ys[i]
+        return inv * first, second
+
+    for r in range(0, rows, 8):
+        for c in range(3):
+            both = combined([strips[i, c, r : r + 8] for i in range(5)], strip_scale[r : r + 8])
+            ends[c, r : r + 8], ends[3 + c, r : r + 8] = both
+    mine = lax.axis_index("gx") * planes
+    lane = lanes_of((8, lanes))
+
     def plane(p, carry):
+        shift = lanes - 8 - (SW * (mine + p) + 4)
         for r in range(0, rows, 8):
             inv = scale[p, r : r + 8]
             for c in range(3):
-                ys = [basis[i, c, p, r : r + 8] for i in range(5)]
-                first = disp[0] * ys[0]
-                second = res[0] * ys[0]
-                for i in range(1, 5):
-                    second = second + res[i] * ys[i]
-                    if i < 4:
-                        first = first + disp[i] * ys[i]
-                displacement[c, p, r : r + 8] = inv * first
-                residual[c, p, r : r + 8] = second
+                both = combined([basis[i, c, p, r : r + 8] for i in range(5)], inv)
+                for n, out in enumerate((displacement, residual)):
+                    end = turned(ends[3 * n + c, r : r + 8], shift, 1)
+                    out[c, p, r : r + 8] = jnp.where(lane < lanes - 8, both[n], end)
         return carry
 
     lax.fori_loop(0, planes, plane, 0)
 
 
-def call(kernel, outs, *args, scratch=()):
-    f32 = lambda shape: jax.ShapeDtypeStruct(shape, jnp.float32)
+def call(kernel, outs, *args, scratch=(), space=pltpu.VMEM):
     return pl.pallas_call(
         kernel,
-        out_shape=tuple(f32(shape) for shape in outs),
-        in_specs=[pl.BlockSpec(memory_space=pltpu.VMEM)] * len(args),
+        out_shape=tuple(jax.ShapeDtypeStruct(shape, jnp.float32) for shape in outs),
+        in_specs=[pl.BlockSpec(memory_space=space)] * len(args),
         out_specs=tuple(pl.BlockSpec(memory_space=pltpu.VMEM) for _ in outs),
-        scratch_shapes=[pltpu.VMEM(shape, jnp.float32) for shape in scratch],
+        scratch_shapes=list(scratch),
         compiler_params=pltpu.CompilerParams(vmem_limit_bytes=VMEM_LIMIT),
     )(*args)
 
 
-def swapped(value, axis, first):
+def swapped(value, axis, first, across=False):
     count = lax.axis_size(axis)
     pairs = [(i, i + 1) for i in range(first, count - 1, 2)]
+    pairs = pairs + [(j, i) for i, j in pairs]
     if not pairs:
         return jnp.zeros_like(value)
-    return lax.ppermute(value, axis, pairs + [(j, i) for i, j in pairs])
+    if not across:
+        return lax.ppermute(value, axis, pairs)
+    return lax.ppermute(value, ("gx", axis), [(x * count + i, (1 - x) * count + j) for x in range(2) for i, j in pairs])
 
 
 def paired_shards(density, fixed_mask, load_mask, load_values):
@@ -816,56 +846,54 @@
     grid = (rows * lax.axis_size("gy"), lanes * lax.axis_size("gz"))
     count = 2 * planes
     wide, tall = rows + 2 * FACE, rows + FACE
-    face = (5 * planes, FACE, lanes)
-    strips = (wide + 2 * tall, lanes)
+    face, bare = (5 * planes, FACE, lanes), (planes, FACE, lanes)
     row = (devices, 1, lanes)
-    fields, send_a, send_b = call(
-        pack_kernel, ((5 * planes, rows, lanes), face, face), density, fixed_mask, load_mask, load_values
+    f32, i32 = jnp.float32, jnp.int32
+    density_other = swapped(density, "gx", 0)
+    send_a, send_b, bare_a, bare_b = call(
+        face_kernel, (face, face, bare, bare), density, fixed_mask, load_mask, load_values, space=pl.ANY,
+        scratch=(
+            pltpu.VMEM((2,) + bare, f32), pltpu.VMEM((2,) + bare, i32), pltpu.VMEM((2,) + bare, i32),
+            pltpu.VMEM((2, 3) + bare, f32), pltpu.SemaphoreType.DMA((8,)),
+        ),
     )
-    density_own, node_own, own, send_a, send_b = call(
+    window, nodes, strips = call(
         strip_kernel,
-        ((planes, wide, lanes), (4 * planes, tall, lanes), strips, strips, strips),
-        fields, swapped(send_a, "gy", 0), swapped(send_b, "gy", 1),
+        ((count, wide, lanes), (4 * planes, tall, lanes), (wide + 2 * tall, lanes)),
+        density, density_other, fixed_mask, load_mask, load_values,
+        swapped(send_a, "gy", 0), swapped(send_b, "gy", 1),
+        swapped(bare_a, "gy", 0, True), swapped(bare_b, "gy", 1, True),
     )
-    density_other = swapped(density_own, "gx", 0)
-    node_other = swapped(node_own, "gx", 0)
-    strip_own = own + swapped(send_a, "gz", 0) + swapped(send_b, "gz", 1)
-    strip_other = swapped(strip_own, "gx", 0)
-    window, first, strip_v, strip_g, dots = call(
+    from_a, from_b = swapped(strips, "gz", 0), swapped(strips, "gz", 1)
+    nodes_other = swapped(nodes, "gx", 0)
+    first, strip_v, strip_g, node_strips, dots = call(
         functools.partial(filter_kernel, grid),
-        ((count, wide, lanes), (count, wide, lanes), (wide, lanes), (wide, lanes), row),
-        density_own, density_other, strip_own, strip_other,
+        ((count, wide, lanes), (wide, lanes), (wide, lanes), (4 * tall, lanes), row),
+        window, strips, from_a, from_b,
+    )
+    strips_other = swapped(node_strips, "gx", 0)
+    dots = lax.all_to_all(dots, AXES, 0, 0, tiled=True)
+    diagonal = float(element_table()[0, 0, 0, 0])
+    plane, taller = (tall, lanes), (tall + 8, lanes)
+    many = (count,) + plane
+    filtered, basis, strip_basis, scale, strip_scale, dots = call(
+        functools.partial(solve_kernel, grid, diagonal),
+        ((planes, rows, lanes), (5, 3, planes, rows, lanes), (5, 3, rows, lanes), (planes, rows, lanes), (rows, lanes), row),
+        window, first, strip_v, strip_g, dots, nodes, nodes_other, node_strips, strips_other,
+        scratch=[
+            pltpu.VMEM(shape, f32)
+            for shape in (
+                (5, 3) + many, many, many, many, (6, count + 1) + taller, (12,) + plane, (12,) + plane, (6,) + plane, (6,) + taller,
+                (5, 3) + plane, plane, plane, plane, (12,) + taller, (12,) + plane, (12,) + taller, (6,) + plane, (3,) + plane,
+            )
+        ],
     )
     dots = lax.all_to_all(dots, AXES, 0, 0, tiled=True)
-    table = element_table()
-    diagonal = float(table[0, 0, 0, 0])
-    plane = (tall, lanes)
-    filtered, basis, scale, dots = call(
-        functools.partial(solve_wrapped, grid, diagonal),
-        ((planes, rows, lanes), (5, 3, planes, rows, lanes), (planes, rows, lanes), row),
-        window, first, strip_v, strip_g, dots, node_own, node_other, strip_own, strip_other,
-        scratch=(
-            (5, 3, count) + plane,
-            (count,) + plane, (count,) + plane, (count,) + plane,
-            (6, count + 1, tall + 8, lanes), (12,) + plane, (12,) + plane, (6,) + plane, (6, tall + 8, lanes),
-            (1,) + plane, plane, plane, (3,) + plane, (4, 3, tall + 8, lanes), (6,) + plane, (6, tall + 8, lanes),
-            (4, 3) + plane,
-        ),
+    displacement, residual = call(
+        combine_kernel, (load_values.shape, load_values.shape), dots, basis, strip_basis, scale, strip_scale,
+        scratch=[pltpu.VMEM((6, rows, lanes), f32)],
     )
-    dots = lax.all_to_all(dots, AXES, 0, 0, tiled=True)
-    displacement, residual = call(combine_kernel, (load_values.shape, load_values.shape), dots, basis, scale)
     return (filtered, displacement, residual)
-
-
-def solve_wrapped(
-    grid, diagonal, window, first, strip_v, strip_g, filter_dots, node_own, node_other, strip_own, strip_other,
-    filtered, fields, scale, dots, basis, modulus, inverse, free, pairs, kept, carried, near, far, *strip_scratch,
-):
-    solve_kernel(
-        grid, diagonal, window, first, strip_v, strip_g, filter_dots, node_own, node_other, strip_own, strip_other,
-        filtered, basis, scale, dots,
-        modulus, inverse, free, fields, pairs, kept, carried, near, far, *strip_scratch,
-    )
 
 
 def shards(density, fixed_mask, load_mask, load_values):

time: 83 us -> 64.2 us (0.77)
  Pallas kernels: 31.8 us -> 18 us
  waiting for transfers between devices: 12.8 us -> 3.57 us
  starting transfers between devices: 7.05 us -> 14.7 us
  blocking collectives: 26.7 us -> 23.3 us
    pallas_call x5, Pallas kernels: 31.8 us -> 18 us  [call(): pl.pallas_call(kernel, out_shape=tuple((jax.ShapeDtypeStruct(shape, jnp.f...]
    ppermute x7 -> x9, waiting for transfers between devices: 12.8 us -> 3.57 us  [the longest x7 2.78 us: swapped(): return lax.ppermute(value, axis, pairs)]
    ppermute x7 -> x9, starting transfers between devices: 7.05 us -> 14.7 us  [the longest x7 11 us: swapped(): return lax.ppermute(value, axis, pairs)]
    all_to_all x2, blocking collectives: 26.7 us -> 23.3 us  [paired_shards(): dots = lax.all_to_all(dots, AXES, 0, 0, tiled=True)]
  transfers between devices with their start and end apart: 7 -> 9, of which waited for: 4 -> 2; matrix products, arithmetic and copies ran while one was open for 0% -> 0% of each run, Pallas kernels for 2% -> 3%
where the time goes in v2:
time: 64.2 us; the launch traced here: 64 us
  blocking collectives  23.3 us (36%)
  Pallas kernels  18 us (28%)
  starting transfers between devices  14.7 us (23%)
  local copies, waits for them, and re-layouts  3.71 us (6%)
  waiting for transfers between devices  3.57 us (6%)
  between operations  0.71 us (1%)
    all_to_all x2, blocking collectives, paired_shards(): dots = lax.all_to_all(dots, AXES, 0, 0, tiled=True)  23.3 us
    pallas_call x5, Pallas kernels, call(): pl.pallas_call(kernel, out_shape=tuple((jax.ShapeDtypeStruct(shape, jnp.f...  18 us
    ppermute x7, starting transfers between devices, swapped(): return lax.ppermute(value, axis, pairs)  11 us
    unnamed x8, local copies, waits for them, and re-layouts  3.71 us
    ppermute x2, starting transfers between devices, swapped(): lax.ppermute(value, ('gx', axis), [(x * count + i, (1 - x) * count + j) f...  3.68 us
    ppermute x7, waiting for transfers between devices, swapped(): return lax.ppermute(value, axis, pairs)  2.78 us
  transfers between devices with their start and end apart: 9, of which 2 were waited for; matrix products, arithmetic and copies ran while one was open for 0% of the time, Pallas kernels for 3%

profile of v2, /device:TPU:0, one launch (start us, length us, event | category | flops | bytes accessed | tf_op | source)
XLA Modules:
  0.0 64.0 jit_solution(17453054574812477687)
XLA Ops:
  0.6 3.0 %collective-permute-start = (f32[4,64,128]{2,1,0:T(8,128)}, f32[4,64,128]{2,1,0:T(8,128)S(1)}, u32[]{:S(2)}, u32[]{:S(2)}) collective-permute-start(f32[4,64,128]{2,1,0:T(8,128)} %density.3), channel_id=1, source_target_pairs={{0,16},{16,0},{1,17},{17,1},{2,18},{18,2},{3,19},{19,3},{4,20},{20... | collective-permute-start | bytes 393224 | tf_op jit(solution)/shard_map/ppermute | solution.py:837
  3.7 0.0 copy-start
  3.7 1.0 %copy-done = f32[3,4,64,128]{3,2,1,0:T(8,128)S(1)} copy-done((f32[3,4,64,128]{3,2,1,0:T(8,128)S(1)}, f32[3,4,64,128]{3,2,1,0:T(8,128)}, u32[]{:S(2)}) %copy-start) | copy-done | bytes 393240
  4.7 0.0 copy-start.1
  4.7 0.9 %copy-done.1 = f32[4,64,128]{2,1,0:T(8,128)S(1)} copy-done((f32[4,64,128]{2,1,0:T(8,128)S(1)}, f32[4,64,128]{2,1,0:T(8,128)}, u32[]{:S(2)}) %copy-start.1) | copy-done | bytes 131096
  5.6 0.0 copy-start.2
  5.6 0.9 %copy-done.2 = s32[4,64,128]{2,1,0:T(8,128)S(1)} copy-done((s32[4,64,128]{2,1,0:T(8,128)S(1)}, s32[4,64,128]{2,1,0:T(8,128)}, u32[]{:S(2)}) %copy-start.2) | copy-done | bytes 131096
  6.5 0.0 copy-start.3
  6.5 0.9 %copy-done.3 = s32[4,64,128]{2,1,0:T(8,128)S(1)} copy-done((s32[4,64,128]{2,1,0:T(8,128)S(1)}, s32[4,64,128]{2,1,0:T(8,128)}, u32[]{:S(2)}) %copy-start.3) | copy-done | bytes 131096
  7.4 0.1 shard_map.67
  7.5 0.1 collective-permute-start.1
  7.6 0.7 %collective-permute-start.2 = (f32[20,8,128]{2,1,0:T(8,128)S(1)}, f32[20,8,128]{2,1,0:T(8,128)S(1)}, u32[]{:S(2)}, u32[]{:S(2)}) collective-permute-start(f32[20,8,128]{2,1,0:T(8,128)S(1)} %get-tuple-element.24), channel_id=1, source_target_pairs={{4,8},{8,4},{5,9},{9,5},{6,10},{10,6},{7,11},{11,7},{20,24},{24,20... | collective-permute-start | bytes 245768 | tf_op jit(solution)/shard_map/ppermute | solution.py:837
  8.3 3.0 %collective-permute-start.3 = (f32[4,8,128]{2,1,0:T(8,128)S(1)}, f32[4,8,128]{2,1,0:T(8,128)S(1)}, u32[]{:S(2)}, u32[]{:S(2)}) collective-permute-start(f32[4,8,128]{2,1,0:T(8,128)S(1)} %get-tuple-element.25), channel_id=1, source_target_pairs={{0,20},{8,28},{4,16},{12,24},{16,4},{24,12},{20,0},{28,8},{1,21},{... | collective-permute-start | bytes 49160 | tf_op jit(solution)/shard_map/ppermute | solution.py:838
  11.3 0.7 %collective-permute-start.4 = (f32[4,8,128]{2,1,0:T(8,128)S(1)}, f32[4,8,128]{2,1,0:T(8,128)S(1)}, u32[]{:S(2)}, u32[]{:S(2)}) collective-permute-start(f32[4,8,128]{2,1,0:T(8,128)S(1)} %get-tuple-element.26), channel_id=1, source_target_pairs={{4,24},{8,20},{20,8},{24,4},{5,25},{9,21},{21,9},{25,5},{6,26},{10... | collective-permute-start | bytes 49160 | tf_op jit(solution)/shard_map/ppermute | solution.py:838
  12.0 0.8 %collective-permute-done.3.bare_a = f32[4,8,128]{2,1,0:T(8,128)S(1)} collective-permute-done((f32[4,8,128]{2,1,0:T(8,128)S(1)}, f32[4,8,128]{2,1,0:T(8,128)S(1)}, u32[]{:S(2)}, u32[]{:S(2)}) %collective-permute-start.3) | collective-permute-done | bytes 16416 | tf_op jit(solution)/shard_map/ppermute | solution.py:838
  12.8 0.0 collective-permute-done.4.bare_b
  12.8 0.0 collective-permute-done.1.from_a
  12.8 0.0 collective-permute-done.2.from_b
  12.8 0.0 collective-permute-done.other
  12.8 0.3 shard_map.68
  13.1 1.6 %collective-permute-start.7 = (f32[16,72,128]{2,1,0:T(8,128)S(1)}, f32[16,72,128]{2,1,0:T(8,128)S(1)}, u32[]{:S(2)}, u32[]{:S(2)}) collective-permute-start(f32[16,72,128]{2,1,0:T(8,128)S(1)} %get-tuple-element.33.node_own), channel_id=1, source_target_pairs={{0,16},{16,0},{1,17},{17,1},{2,18},{18,2},{3,19},{19,3},{4,20},{20... | collective-permute-start | bytes 1769480 | tf_op jit(solution)/shard_map/ppermute | solution.py:837
  14.7 0.7 %collective-permute-start.6 = (f32[224,128]{1,0:T(8,128)S(1)}, f32[224,128]{1,0:T(8,128)S(1)}, u32[]{:S(2)}, u32[]{:S(2)}) collective-permute-start(f32[224,128]{1,0:T(8,128)S(1)} %get-tuple-element.28.strips), channel_id=1, source_target_pairs={{1,2},{2,1},{5,6},{6,5},{9,10},{10,9},{13,14},{14,13},{17,18},{18,... | collective-permute-start | bytes 344072 | tf_op jit(solution)/shard_map/ppermute | solution.py:837
  15.4 4.5 %collective-permute-start.5 = (f32[224,128]{1,0:T(8,128)S(1)}, f32[224,128]{1,0:T(8,128)S(1)}, u32[]{:S(2)}, u32[]{:S(2)}) collective-permute-start(f32[224,128]{1,0:T(8,128)S(1)} %get-tuple-element.28.strips), channel_id=1, source_target_pairs={{0,1},{2,3},{1,0},{3,2},{4,5},{6,7},{5,4},{7,6},{8,9},{10,11},{9,8... | collective-permute-start | bytes 344072 | tf_op jit(solution)/shard_map/ppermute | solution.py:837
  19.8 0.0 collective-permute-done.6.from_b
  19.8 2.8 %collective-permute-done.5.from_a = f32[224,128]{1,0:T(8,128)S(1)} collective-permute-done((f32[224,128]{1,0:T(8,128)S(1)}, f32[224,128]{1,0:T(8,128)S(1)}, u32[]{:S(2)}, u32[]{:S(2)}) %collective-permute-start.5) | collective-permute-done | bytes 114720 | tf_op jit(solution)/shard_map/ppermute | solution.py:837
  22.6 1.8 %shard_map.69 = (f32[8,80,128]{2,1,0:T(8,128)S(1)}, f32[80,128]{1,0:T(8,128)S(1)}, f32[80,128]{1,0:T(8,128)S(1)}, f32[288,128]{1,0:T(8,128)S(1)}, f32[32,1,128]{2,1,0:T(1,128)S(1)}) custom-call(f32[8,80,128]{2,1,0:T(8,128)S(1)} %get-tuple-element.27.window, f32[224,128]{1,0:T(8,128)S(1)} %get-tuple-element.28.strips, ...), custom_call_target="tpu_custom_call" | custom-call | tf_op jit(solution)/shard_map/pallas_call | solution.py:820
  24.4 0.6 collective-permute-start.8
  25.0 13.8 %all_to_all.10.filter_dots = f32[32,1,128]{2,1,0:T(1,128)S(1)} all-to-all(f32[32,1,128]{2,1,0:T(1,128)S(1)} %get-tuple-element.32), channel_id=1, replica_groups=mesh['gx'=2,'gy'=4,'gz'=4] {'gx','gy','gz'}, dimensions={0} | all-to-all | bytes 32768 | tf_op jit(solution)/shard_map/all_to_all | solution.py:875
  38.8 0.0 collective-permute-done.8.strip_other
  38.8 0.0 collective-permute-done.7.node_other
  38.8 14.1 %shard_map.70 = (f32[4,64,128]{2,1,0:T(8,128)}, f32[5,3,4,64,128]{4,3,2,1,0:T(8,128)S(1)}, f32[5,3,64,128]{3,2,1,0:T(8,128)S(1)}, f32[4,64,128]{2,1,0:T(8,128)S(...) custom-call(f32[8,80,128]{2,1,0:T(8,128)S(1)} %get-tuple-element.27.window, ...), custom_call_target="tpu_custom_call" | custom-call | tf_op jit(solution)/shard_map/pallas_call | solution.py:820
  52.9 9.5 %all_to_all.11.dots = f32[32,1,128]{2,1,0:T(1,128)S(1)} all-to-all(f32[32,1,128]{2,1,0:T(1,128)S(1)} %get-tuple-element.36), channel_id=1, replica_groups=mesh['gx'=2,'gy'=4,'gz'=4] {'gx','gy','gz'}, dimensions={0} | all-to-all | bytes 32768 | tf_op jit(solution)/shard_map/all_to_all | solution.py:891
  62.3 1.6 %shard_map.71 = (f32[3,4,64,128]{3,2,1,0:T(8,128)}, f32[3,4,64,128]{3,2,1,0:T(8,128)}) custom-call(f32[32,1,128]{2,1,0:T(1,128)S(1)} %all_to_all.11.dots, f32[5,3,4,64,128]{4,3,2,1,0:T(8,128)S(1)} %get-tuple-element.37.basis, f32[5,3,64,128]{3,2,1,0:T(8,128)S(1)} %get-tuple-element.38.strips, f32[4,64,128]{2,1,0:T(8,128)S(1)} %get-tuple-element.39.scale, ...), custom_call_target="tpu_custom_call" | custom-call | tf_op jit(solution)/shard_map/pallas_call | solution.py:820
Async XLA Ops:
  0.6 12.1 %collective-permute-start = (f32[4,64,128]{2,1,0:T(8,128)}, f32[4,64,128]{2,1,0:T(8,128)S(1)}, u32[]{:S(2)}, u32[]{:S(2)}) collective-permute-start(f32[4,64,128]{2,1,0:T(8,128)} %density.3), channel_id=1, source_target_pairs={{0,16},{16,0},{1,17},{17,1},{2,18},{18,2},{3,19},{19,3},{4,20},{20... | collective-permute-start | bytes 393224 | tf_op jit(solution)/shard_map/ppermute | solution.py:837
  3.7 1.0 %copy-start = (f32[3,4,64,128]{3,2,1,0:T(8,128)S(1)}, f32[3,4,64,128]{3,2,1,0:T(8,128)}, u32[]{:S(2)}) copy-start(f32[3,4,64,128]{3,2,1,0:T(8,128)} %load_values.3) | copy-start | bytes 1179652
  4.7 0.9 %copy-start.1 = (f32[4,64,128]{2,1,0:T(8,128)S(1)}, f32[4,64,128]{2,1,0:T(8,128)}, u32[]{:S(2)}) copy-start(f32[4,64,128]{2,1,0:T(8,128)} %density.3) | copy-start | bytes 393220
  5.6 0.9 %copy-start.2 = (s32[4,64,128]{2,1,0:T(8,128)S(1)}, s32[4,64,128]{2,1,0:T(8,128)}, u32[]{:S(2)}) copy-start(s32[4,64,128]{2,1,0:T(8,128)} %fixed.3) | copy-start | bytes 393220
  6.5 0.9 %copy-start.3 = (s32[4,64,128]{2,1,0:T(8,128)S(1)}, s32[4,64,128]{2,1,0:T(8,128)}, u32[]{:S(2)}) copy-start(s32[4,64,128]{2,1,0:T(8,128)} %load_mask.3) | copy-start | bytes 393220
  7.5 5.2 %collective-permute-start.1 = (f32[20,8,128]{2,1,0:T(8,128)S(1)}, f32[20,8,128]{2,1,0:T(8,128)S(1)}, u32[]{:S(2)}, u32[]{:S(2)}) collective-permute-start(f32[20,8,128]{2,1,0:T(8,128)S(1)} %get-tuple-element.23), channel_id=1, source_target_pairs={{0,4},{8,12},{4,0},{12,8},{1,5},{9,13},{5,1},{13,9},{2,6},{10,14},... | collective-permute-start | bytes 245768 | tf_op jit(solution)/shard_map/ppermute | solution.py:837
  7.6 5.2 %collective-permute-start.2 = (f32[20,8,128]{2,1,0:T(8,128)S(1)}, f32[20,8,128]{2,1,0:T(8,128)S(1)}, u32[]{:S(2)}, u32[]{:S(2)}) collective-permute-start(f32[20,8,128]{2,1,0:T(8,128)S(1)} %get-tuple-element.24), channel_id=1, source_target_pairs={{4,8},{8,4},{5,9},{9,5},{6,10},{10,6},{7,11},{11,7},{20,24},{24,20... | collective-permute-start | bytes 245768 | tf_op jit(solution)/shard_map/ppermute | solution.py:837
  8.3 4.5 %collective-permute-start.3 = (f32[4,8,128]{2,1,0:T(8,128)S(1)}, f32[4,8,128]{2,1,0:T(8,128)S(1)}, u32[]{:S(2)}, u32[]{:S(2)}) collective-permute-start(f32[4,8,128]{2,1,0:T(8,128)S(1)} %get-tuple-element.25), channel_id=1, source_target_pairs={{0,20},{8,28},{4,16},{12,24},{16,4},{24,12},{20,0},{28,8},{1,21},{... | collective-permute-start | bytes 49160 | tf_op jit(solution)/shard_map/ppermute | solution.py:838
  11.3 1.4 %collective-permute-start.4 = (f32[4,8,128]{2,1,0:T(8,128)S(1)}, f32[4,8,128]{2,1,0:T(8,128)S(1)}, u32[]{:S(2)}, u32[]{:S(2)}) collective-permute-start(f32[4,8,128]{2,1,0:T(8,128)S(1)} %get-tuple-element.26), channel_id=1, source_target_pairs={{4,24},{8,20},{20,8},{24,4},{5,25},{9,21},{21,9},{25,5},{6,26},{10... | collective-permute-start | bytes 49160 | tf_op jit(solution)/shard_map/ppermute | solution.py:838
  13.1 25.7 %collective-permute-start.7 = (f32[16,72,128]{2,1,0:T(8,128)S(1)}, f32[16,72,128]{2,1,0:T(8,128)S(1)}, u32[]{:S(2)}, u32[]{:S(2)}) collective-permute-start(f32[16,72,128]{2,1,0:T(8,128)S(1)} %get-tuple-element.33.node_own), channel_id=1, source_target_pairs={{0,16},{16,0},{1,17},{17,1},{2,18},{18,2},{3,19},{19,3},{4,20},{20... | collective-permute-start | bytes 1769480 | tf_op jit(solution)/shard_map/ppermute | solution.py:837
  14.7 5.1 %collective-permute-start.6 = (f32[224,128]{1,0:T(8,128)S(1)}, f32[224,128]{1,0:T(8,128)S(1)}, u32[]{:S(2)}, u32[]{:S(2)}) collective-permute-start(f32[224,128]{1,0:T(8,128)S(1)} %get-tuple-element.28.strips), channel_id=1, source_target_pairs={{1,2},{2,1},{5,6},{6,5},{9,10},{10,9},{13,14},{14,13},{17,18},{18,... | collective-permute-start | bytes 344072 | tf_op jit(solution)/shard_map/ppermute | solution.py:837
  15.4 7.2 %collective-permute-start.5 = (f32[224,128]{1,0:T(8,128)S(1)}, f32[224,128]{1,0:T(8,128)S(1)}, u32[]{:S(2)}, u32[]{:S(2)}) collective-permute-start(f32[224,128]{1,0:T(8,128)S(1)} %get-tuple-element.28.strips), channel_id=1, source_target_pairs={{0,1},{2,3},{1,0},{3,2},{4,5},{6,7},{5,4},{7,6},{8,9},{10,11},{9,8... | collective-permute-start | bytes 344072 | tf_op jit(solution)/shard_map/ppermute | solution.py:837
  24.4 14.4 %collective-permute-start.8 = (f32[288,128]{1,0:T(8,128)S(1)}, f32[288,128]{1,0:T(8,128)S(1)}, u32[]{:S(2)}, u32[]{:S(2)}) collective-permute-start(f32[288,128]{1,0:T(8,128)S(1)} %get-tuple-element.34.strip_own), channel_id=1, source_target_pairs={{0,16},{16,0},{1,17},{17,1},{2,18},{18,2},{3,19},{19,3},{4,20},{20... | collective-permute-start | bytes 442376 | tf_op jit(solution)/shard_map/ppermute | solution.py:837

commit v3 on v2

--- a/solution.py
+++ b/solution.py
@@ -221,7 +221,6 @@
 HALO = 4
 SW = 16
 FACE = 8
-PARTS = 8
 AXES = ("gx", "gy", "gz")
 SHIFTS = (1.2, 0.4, 2.0, 0.8)
 VMEM_LIMIT = 24 * 1024 * 1024
@@ -255,67 +254,70 @@
     return jnp.where(jnp.full(first.shape, flag, jnp.int32) == 0, first, second)
 
 
-def face_kernel(density, fixed, load_mask, load_values, send_a, send_b, bare_a, bare_b, d, f, m, v, done):
-    planes, rows, _ = density.shape
-    copies = []
-    for side, at in ((0, 0), (1, rows - FACE)):
-        for source, target in ((density, d), (fixed, f), (load_mask, m)):
-            copies.append((source.at[:, at : at + FACE, :], target.at[side]))
-        copies.append((load_values.at[:, :, at : at + FACE, :], v.at[side]))
-    copies = [pltpu.make_async_copy(src, dst, done.at[n]) for n, (src, dst) in enumerate(copies)]
-    for copy in copies:
-        copy.start()
-    for copy in copies:
-        copy.wait()
+def node_kernel(density, fixed, load_mask, load_values, held, nodes):
+    planes = density.shape[0]
+    held[...] = density[...]
+    for p in range(planes):
+        free = (1 - fixed[p]).astype(jnp.float32)
+        loaded = free * load_mask[p].astype(jnp.float32)
+        nodes[p] = free
+        for c in range(3):
+            nodes[(1 + c) * planes + p] = loaded * load_values[c, p]
+
+
+def face_kernel(density, other, nodes, send_a, send_b):
+    planes, rows, lanes = density.shape
+    half = 2 * planes
+    gx = lax.axis_index("gx")
     odd = lax.rem(lax.axis_index("gy"), 2)
-    for send, bare, side in ((send_a, bare_a, 1 - odd), (send_b, bare_b, odd)):
-        free = (1 - f[side]).astype(jnp.float32)
-        loaded = free * m[side].astype(jnp.float32)
-        send[:planes] = d[side]
-        bare[...] = d[side]
-        send[planes : 2 * planes] = free
-        for c in range(3):
-            send[(2 + c) * planes : (3 + c) * planes] = loaded * v[side, c]
-
-
-def strip_kernel(
-    density, other, fixed, load_mask, load_values, from_a, from_b, bare_a, bare_b, window, nodes, strips
-):
+    top = rows - FACE
+    row = rows_of((FACE, lanes))
+    for p in range(planes):
+        for source, at in ((density, gx * planes), (other, planes - gx * planes)):
+            low, high = source[p, :FACE], source[p, top:]
+            send_a[at + p] = either(odd, high, low)
+            send_b[at + p] = either(odd, low, high)
+    for q in range(half):
+        low = jnp.where(row < HALO, nodes[q, :FACE], turned(nodes[q + half, :FACE], HALO, 0))
+        high = jnp.where(row < HALO, turned(nodes[q + half, top:], HALO, 0), nodes[q, top:])
+        send_a[half + q] = either(odd, high, low)
+        send_b[half + q] = either(odd, low, high)
+
+
+def strip_kernel(density, other, nodes, from_a, from_b, window, tails, strips):
     planes, rows, lanes = density.shape
     wide, tall = rows + 2 * FACE, rows + FACE
+    half = 2 * planes
     mine = lax.axis_index("gx") * planes
     odd_y = lax.rem(lax.axis_index("gy"), 2)
     row = rows_of((FACE, lanes))
-    for source, a, b, at in ((density, from_a, from_b, mine), (other, bare_a, bare_b, planes - mine)):
+    for source, at in ((density, mine), (other, planes - mine)):
         for p in range(planes):
             window[at + p, :rows] = source[p]
-            window[at + p, rows : rows + FACE] = either(odd_y, a[p], b[p])
-            window[at + p, rows + FACE :] = either(odd_y, b[p], a[p])
-    lane = lanes_of((wide, lanes))
-    packed = jnp.zeros((wide, lanes), jnp.float32)
-    for p in range(2 * planes):
-        packed = jnp.where(lane // SW == p, turned(window[p], SW * p + 8, 1), packed)
-    strips[:wide] = packed
-    for p in range(planes):
-        free = (1 - fixed[p]).astype(jnp.float32)
-        loaded = free * load_mask[p].astype(jnp.float32)
-        nodes[p, :rows] = free
-        for c in range(3):
-            nodes[(1 + c) * planes + p, :rows] = loaded * load_values[c, p]
-    for q in range(4 * planes):
-        above = either(odd_y, from_a[planes + q], from_b[planes + q])
-        below = either(odd_y, from_b[planes + q], from_a[planes + q])
-        nodes[q, rows:] = jnp.where(row < HALO, above, below)
-    lane = lanes_of((tall, lanes))
+    for p in range(half):
+        window[p, rows : rows + FACE] = either(odd_y, from_a[p], from_b[p])
+        window[p, rows + FACE :] = either(odd_y, from_b[p], from_a[p])
+        above = either(odd_y, from_a[half + p], from_b[half + p])
+        below = either(odd_y, from_b[half + p], from_a[half + p])
+        tails[p] = jnp.where(row < HALO, above, below)
+        tails[half + p] = jnp.where(row < HALO, turned(above, HALO, 0), turned(below, HALO, 0))
+    for begin, end in ((0, rows), (rows, wide)):
+        lane = lanes_of((end - begin, lanes))
+        packed = jnp.zeros((end - begin, lanes), jnp.float32)
+        for p in range(half):
+            packed = jnp.where(lane // SW == p, turned(window[p, begin:end], SW * p + 8, 1), packed)
+        strips[begin:end] = packed
     for pair in range(2):
-        packed = jnp.zeros((tall, lanes), jnp.float32)
-        for q in range(2 * planes):
-            value = nodes[2 * planes * pair + q]
-            packed = jnp.where(lane // SW == q, turned(value, SW * q + 12, 1), packed)
-        strips[wide + pair * tall : wide + (pair + 1) * tall] = packed
-
-
-def filter_kernel(grid, window, strips, from_a, from_b, first, strip_v, strip_g, node_strips, dots):
+        at = wide + pair * tall
+        for source, size, begin in ((nodes, rows, at), (tails, FACE, at + rows)):
+            lane = lanes_of((size, lanes))
+            packed = jnp.zeros((size, lanes), jnp.float32)
+            for q in range(half):
+                packed = jnp.where(lane // SW == q, turned(source[half * pair + q], SW * q + 12, 1), packed)
+            strips[begin : begin + size] = packed
+
+
+def filter_kernel(grid, window, tails, strips, from_a, from_b, first, strip_v, strip_g, node_strips, dots):
     count, wide, lanes = window.shape
     rows = wide - 2 * FACE
     planes = count // 2
@@ -343,22 +345,18 @@
         ahead = (turned(value, -1, 0) - value) * pass_y
         return turned(ahead, 1, 0) - ahead
 
-    def laplace(source, strip, p):
+    def laplace(source, side, q, p, lower, upper):
         value = source[p]
-        result = (value - source[jnp.minimum(p + 1, count - 1)]) + (value - source[jnp.maximum(p - 1, 0)])
+        result = (value - source[upper]) + (value - source[lower])
         result = result + along_y(value)
-        side = strip[...]
-        ahead = jnp.where(lane == lanes - 1, turned(side, lanes - 1 - (SW * p + 8), 1), turned(value, -1, 1))
-        behind = jnp.where(lane == 0, turned(side, 0 - (SW * p + 7), 1), turned(value, 1, 1))
+        ahead = jnp.where(lane == lanes - 1, turned(side, lanes - 1 - (SW * q + 8), 1), turned(value, -1, 1))
+        behind = jnp.where(lane == 0, turned(side, 0 - (SW * q + 7), 1), turned(value, 1, 1))
         result = result + (value - ahead) * pass_z + (value - behind) * back_z
         return filter_weight * result
 
-    def first_plane(p, carry):
-        first[p] = laplace(window, strip_v, p)
-        return carry
-
-    lax.fori_loop(0, count, first_plane, 0)
     value = strip_v[...]
+    for p in range(count):
+        first[p] = laplace(window, value, p, p, max(p - 1, 0), min(p + 1, count - 1))
     edge_low = jnp.zeros(shape, jnp.float32)
     edge_high = edge_low
     for p in range(count):
@@ -371,22 +369,23 @@
     result = result + turned(ahead, SW, 1) - ahead
     strip_g[...] = filter_weight * result
 
-    def add_dots(p, sums):
+    value = strip_g[...]
+    value = either(mine, value, turned(value, lanes // 2, 1))
+    sums = [jnp.zeros((8, lanes), jnp.float32)] * 4
+    for p in range(planes):
         plane = mine + p
         w = window[plane][:rows]
         g = first[plane][:rows]
-        gg = laplace(first, strip_g, plane)[:rows]
+        gg = laplace(first, value, p, plane, jnp.maximum(plane - 1, 0), jnp.minimum(plane + 1, count - 1))[:rows]
         terms = (w * w, w * g, g * g, g * gg)
-        return tuple(
-            s + jnp.sum(t.reshape(rows // 8, 8, lanes), axis=0) for s, t in zip(sums, terms)
-        )
-
-    zero = jnp.zeros((8, lanes), jnp.float32)
-    spread(lax.fori_loop(0, planes, add_dots, (zero,) * 4), dots)
-    half = node_strips.shape[0] // 2
+        sums = [s + jnp.sum(t.reshape(rows // 8, 8, lanes), axis=0) for s, t in zip(sums, terms)]
+    spread(sums, dots)
+    half = strips.shape[0] - wide
     place = lax.rem(lanes_of((half, lanes)), SW)
     node_strips[:half] = jnp.where(place < 12, strips[wide:], either(odd_z, from_a[wide:], from_b[wide:]))
-    node_strips[half:] = either(odd_z, from_b[wide:], from_a[wide:])
+    node_strips[half : 2 * half] = either(odd_z, from_b[wide:], from_a[wide:])
+    for q in range(tails.shape[0]):
+        node_strips[2 * half + FACE * q : 2 * half + FACE * (q + 1)] = tails[q]
 
 
 def spread(sums, dots):
@@ -446,13 +445,13 @@
 def solve_kernel(
     grid, diagonal, window, first, strip_v, strip_g, filter_dots, node_own, node_other, strip_own, strip_other,
     filtered, fields, strip_fields, scale, strip_scale, dots,
-    basis, modulus, inverse, free, pairs, kept, carried, near, far,
+    basis_0, basis_1, basis_2, basis_3, basis_4, modulus, inverse, free, pairs, kept, carried, near, far,
     s_basis, s_modulus, s_inverse, s_free, s_pairs, s_near, s_far, s_part, s_disp,
 ):
+    basis = (basis_0, basis_1, basis_2, basis_3, basis_4)
     count, wide, lanes = window.shape
     rows = wide - 2 * FACE
     tall = rows + FACE
-    tiles = tall // 8
     planes = count // 2
     total_y, total_z = grid
     gx = lax.axis_index("gx")
@@ -497,12 +496,14 @@
             for p in range(planes):
                 q = (f % 2) * planes + p
                 begin = (2 + f // 2) * tall
-                before = turned(strip[begin : begin + tall], lanes - HALO - (SW * q + 8), 1)
-                value = jnp.where(tall_lane < lanes - HALO, source[f * planes + p], before)
-                if f == 0:
-                    free[at + p] = value
-                else:
-                    basis[0, f - 1, at + p] = value
+                tail = 4 * tall + FACE * (f * planes + p)
+                for value, r, n in ((source[f * planes + p], 0, rows), (strip[tail : tail + FACE], rows, FACE)):
+                    before = turned(strip[begin + r : begin + r + n], lanes - HALO - (SW * q + 8), 1)
+                    value = jnp.where(lanes_of((n, lanes)) < lanes - HALO, value, before)
+                    if f == 0:
+                        free[at + p, r : r + n] = value
+                    else:
+                        basis_0[f - 1, at + p, r : r + n] = value
     half = lanes // 2
     left = tall_lane < half
     for pair in range(2):
@@ -535,14 +536,15 @@
         inverse[p, :rows] = inverted(head, free[p, :rows])
         inverse[p, rows:] = inverted(tail, free[p, rows:])
         inside = (lane // SW == p) & (place < 12)
-        s_mod = jnp.where(inside, turned(mod, SW * p + 12, 1), s_mod)
-        s_back = jnp.where(inside, turned(mod, SW * p + 13, 1), s_back)
+        moved = turned(mod, SW * p + 12, 1)
+        s_mod = jnp.where(inside, moved, s_mod)
+        s_back = jnp.where(lane == (SW * p - 1) % lanes, moved, s_back)
     for p in range(planes):
         filtered[p] = (weight_v * window[mine + p] + weight_g * first[mine + p])[:rows]
     head, tail = folded(s_mod)
     s_modulus[:rows] = head
     s_modulus[rows:] = tail
-    across = s_mod + jnp.where(place < 12, s_back, turned(s_mod, 1, 1))
+    across = s_mod + turned(jnp.where(place == SW - 1, s_back, s_mod), 1, 1)
     across = across + turned(across, 1, 0)
     across = across + jnp.where(lane < SW, 0.0, turned(across, SW, 1))
     head, tail = folded(across)
@@ -635,7 +637,7 @@
     def start_plane(p, carry):
         for r in starts:
             for c in range(3):
-                spread_z(c, p, r, inverse[p, r : r + 8] * basis[0, c, p, r : r + 8])
+                spread_z(c, p, r, inverse[p, r : r + 8] * basis_0[c, p, r : r + 8])
         close_rows(p)
         return carry
 
@@ -658,7 +660,7 @@
                     kept[2 * k + beta_, r : r + 8] = both[beta_]
                     carried[2 * k + beta_, r : r + 8] = jnp.zeros((8, lanes), jnp.float32)
 
-        def layer(p, state, j=j):
+        def layer(p, state, j=j, low=low):
             for r in starts:
                 upper_rows = along_rows(p + 1, r)
                 u = []
@@ -693,19 +695,29 @@
                         far[2 * c + g, r + 8 : r + 16] = t_beta[0] + t_beta[1]
             for k in range(6):
                 far[k, 7:8] = far[k, tall + 7 : tall + 8]
-            for r in starts:
-                open_nodes = free[p, r : r + 8]
-                inv = inverse[p, r : r + 8]
-                for c in range(3):
-                    total = near[2 * c, r : r + 8] + far[2 * c, r + 7 : r + 15]
-                    diff = near[2 * c + 1, r : r + 8] + far[2 * c + 1, r + 7 : r + 15]
-                    out = (total - diff) + turned(total + diff, 1, 1)
-                    new = open_nodes * out - SHIFTS[j] * basis[j, c, p, r : r + 8]
-                    basis[j + 1, c, p, r : r + 8] = new
-                    if j < 3:
-                        spread_z(c, p, r, inv * new)
-            if j < 3:
-                close_rows(p)
+            @pl.when((p > low) | (gx == 0))
+            def finish():
+                fresh = {}
+                for r in starts:
+                    open_nodes = free[p, r : r + 8]
+                    for c in range(3):
+                        total = near[2 * c, r : r + 8] + far[2 * c, r + 7 : r + 15]
+                        diff = near[2 * c + 1, r : r + 8] + far[2 * c + 1, r + 7 : r + 15]
+                        out = (total - diff) + turned(total + diff, 1, 1)
+                        fresh[r, c] = open_nodes * out - SHIFTS[j] * basis[j][c, p, r : r + 8]
+                for r in starts:
+                    for c in range(3):
+                        basis[j + 1][c, p, r : r + 8] = fresh[r, c]
+                        if j < 3:
+                            fresh[r, c] = inverse[p, r : r + 8] * fresh[r, c]
+                if j < 3:
+                    ahead = {key: turned(value, -1, 1) for key, value in fresh.items()}
+                    for (r, c), value in fresh.items():
+                        pairs[2 * c, p, r : r + 8] = value + ahead[r, c]
+                        pairs[2 * c + 1, p, r : r + 8] = ahead[r, c] - value
+                if j < 3:
+                    close_rows(p)
+
             return state
 
         lax.fori_loop(low, high, layer, 0)
@@ -720,7 +732,7 @@
             inv = inverse[plane, r : r + 8]
             scale[p, r : r + 8] = inv
             for c in range(3):
-                ys = [basis[i, c, plane, r : r + 8] for i in range(5)]
+                ys = [basis[i][c, plane, r : r + 8] for i in range(5)]
                 ws = [inv * y for y in ys[:4]]
                 for i in range(5):
                     fields[i, c, p, r : r + 8] = ys[i]
@@ -795,47 +807,40 @@
                 first = first + disp[i] * ys[i]
         return inv * first, second
 
+    gx = lax.axis_index("gx")
     for r in range(0, rows, 8):
         for c in range(3):
             both = combined([strips[i, c, r : r + 8] for i in range(5)], strip_scale[r : r + 8])
-            ends[c, r : r + 8], ends[3 + c, r : r + 8] = both
-    mine = lax.axis_index("gx") * planes
+            for n, value in enumerate(both):
+                ends[3 * n + c, r : r + 8] = either(gx, value, turned(value, lanes // 2, 1))
     lane = lanes_of((8, lanes))
-
-    def plane(p, carry):
-        shift = lanes - 8 - (SW * (mine + p) + 4)
+    for p in range(planes):
         for r in range(0, rows, 8):
             inv = scale[p, r : r + 8]
             for c in range(3):
                 both = combined([basis[i, c, p, r : r + 8] for i in range(5)], inv)
                 for n, out in enumerate((displacement, residual)):
-                    end = turned(ends[3 * n + c, r : r + 8], shift, 1)
+                    end = turned(ends[3 * n + c, r : r + 8], lanes - 8 - (SW * p + 4), 1)
                     out[c, p, r : r + 8] = jnp.where(lane < lanes - 8, both[n], end)
-        return carry
-
-    lax.fori_loop(0, planes, plane, 0)
-
-
-def call(kernel, outs, *args, scratch=(), space=pltpu.VMEM):
+
+
+def call(kernel, outs, *args, scratch=()):
     return pl.pallas_call(
         kernel,
         out_shape=tuple(jax.ShapeDtypeStruct(shape, jnp.float32) for shape in outs),
-        in_specs=[pl.BlockSpec(memory_space=space)] * len(args),
+        in_specs=[pl.BlockSpec(memory_space=pltpu.VMEM)] * len(args),
         out_specs=tuple(pl.BlockSpec(memory_space=pltpu.VMEM) for _ in outs),
         scratch_shapes=list(scratch),
         compiler_params=pltpu.CompilerParams(vmem_limit_bytes=VMEM_LIMIT),
     )(*args)
 
 
-def swapped(value, axis, first, across=False):
+def swapped(value, axis, first):
     count = lax.axis_size(axis)
     pairs = [(i, i + 1) for i in range(first, count - 1, 2)]
-    pairs = pairs + [(j, i) for i, j in pairs]
     if not pairs:
         return jnp.zeros_like(value)
-    if not across:
-        return lax.ppermute(value, axis, pairs)
-    return lax.ppermute(value, ("gx", axis), [(x * count + i, (1 - x) * count + j) for x in range(2) for i, j in pairs])
+    return lax.ppermute(value, axis, pairs + [(j, i) for i, j in pairs])
 
 
 def paired_shards(density, fixed_mask, load_mask, load_values):
@@ -846,30 +851,25 @@
     grid = (rows * lax.axis_size("gy"), lanes * lax.axis_size("gz"))
     count = 2 * planes
     wide, tall = rows + 2 * FACE, rows + FACE
-    face, bare = (5 * planes, FACE, lanes), (planes, FACE, lanes)
+    face = (4 * planes, FACE, lanes)
     row = (devices, 1, lanes)
-    f32, i32 = jnp.float32, jnp.int32
+    f32 = jnp.float32
     density_other = swapped(density, "gx", 0)
-    send_a, send_b, bare_a, bare_b = call(
-        face_kernel, (face, face, bare, bare), density, fixed_mask, load_mask, load_values, space=pl.ANY,
-        scratch=(
-            pltpu.VMEM((2,) + bare, f32), pltpu.VMEM((2,) + bare, i32), pltpu.VMEM((2,) + bare, i32),
-            pltpu.VMEM((2, 3) + bare, f32), pltpu.SemaphoreType.DMA((8,)),
-        ),
+    density_own, nodes = call(
+        node_kernel, (density.shape, (4 * planes, rows, lanes)), density, fixed_mask, load_mask, load_values
     )
-    window, nodes, strips = call(
+    nodes_other = swapped(nodes, "gx", 0)
+    send_a, send_b = call(face_kernel, (face, face), density_own, density_other, nodes)
+    window, tails, strips = call(
         strip_kernel,
-        ((count, wide, lanes), (4 * planes, tall, lanes), (wide + 2 * tall, lanes)),
-        density, density_other, fixed_mask, load_mask, load_values,
-        swapped(send_a, "gy", 0), swapped(send_b, "gy", 1),
-        swapped(bare_a, "gy", 0, True), swapped(bare_b, "gy", 1, True),
+        ((count, wide, lanes), (4 * planes, FACE, lanes), (wide + 2 * tall, lanes)),
+        density_own, density_other, nodes, swapped(send_a, "gy", 0), swapped(send_b, "gy", 1),
     )
     from_a, from_b = swapped(strips, "gz", 0), swapped(strips, "gz", 1)
-    nodes_other = swapped(nodes, "gx", 0)
     first, strip_v, strip_g, node_strips, dots = call(
         functools.partial(filter_kernel, grid),
-        ((count, wide, lanes), (wide, lanes), (wide, lanes), (4 * tall, lanes), row),
-        window, strips, from_a, from_b,
+        ((count, wide, lanes), (wide, lanes), (wide, lanes), (4 * tall + 4 * planes * FACE, lanes), row),
+        window, tails, strips, from_a, from_b,
     )
     strips_other = swapped(node_strips, "gx", 0)
     dots = lax.all_to_all(dots, AXES, 0, 0, tiled=True)
@@ -883,7 +883,7 @@
         scratch=[
             pltpu.VMEM(shape, f32)
             for shape in (
-                (5, 3) + many, many, many, many, (6, count + 1) + taller, (12,) + plane, (12,) + plane, (6,) + plane, (6,) + taller,
+                *(((3,) + many,) * 5), many, many, many, (6, count + 1) + taller, (12,) + plane, (12,) + plane, (6,) + plane, (6,) + taller,
                 (5, 3) + plane, plane, plane, plane, (12,) + taller, (12,) + plane, (12,) + taller, (6,) + plane, (3,) + plane,
             )
         ],

time: 64.2 us -> 58.4 us (0.910)
  starting transfers between devices: 14.7 us -> 11 us
  Pallas kernels: 18 us -> 15.9 us
    ppermute x9 -> x7, starting transfers between devices: 14.7 us -> 11 us  [swapped(): return lax.ppermute(value, axis, pairs + [(j, i) for i, j in pairs])]
    pallas_call x5 -> x6, Pallas kernels: 18 us -> 15.9 us  [call(): pl.pallas_call(kernel, out_shape=tuple((jax.ShapeDtypeStruct(shape, jnp.f...]
    ppermute x9 -> x7, waiting for transfers between devices: 3.57 us -> 3.35 us  [swapped(): return lax.ppermute(value, axis, pairs + [(j, i) for i, j in pairs])]
  transfers between devices with their start and end apart: 9 -> 7, of which waited for: 2 -> 2; matrix products, arithmetic and copies ran while one was open for 0% -> 0% of each run, Pallas kernels for 3% -> 2%
where the time goes in v3:
time: 58.4 us; the launch traced here: 58.2 us
  blocking collectives  23.5 us (40%)
  Pallas kernels  15.9 us (27%)
  starting transfers between devices  11 us (19%)
  local copies, waits for them, and re-layouts  3.71 us (6%)
  waiting for transfers between devices  3.35 us (6%)
  between operations  0.69 us (1%)
    all_to_all x2, blocking collectives, paired_shards(): dots = lax.all_to_all(dots, AXES, 0, 0, tiled=True)  23.5 us
    pallas_call x6, Pallas kernels, call(): pl.pallas_call(kernel, out_shape=tuple((jax.ShapeDtypeStruct(shape, jnp.f...  15.9 us
    ppermute x7, starting transfers between devices, swapped(): return lax.ppermute(value, axis, pairs + [(j, i) for i, j in pairs])  11 us
    unnamed x8, local copies, waits for them, and re-layouts  3.71 us
    ppermute x7, waiting for transfers between devices, swapped(): return lax.ppermute(value, axis, pairs + [(j, i) for i, j in pairs])  3.35 us
  transfers between devices with their start and end apart: 7, of which 2 were waited for; matrix products, arithmetic and copies ran while one was open for 0% of the time, Pallas kernels for 2%

profile of v3, /device:TPU:0, one launch (start us, length us, event | category | flops | bytes accessed | tf_op | source)
XLA Modules:
  0.0 58.2 jit_solution(3081453551534170607)
XLA Ops:
  0.6 3.0 %collective-permute-start = (f32[4,64,128]{2,1,0:T(8,128)}, f32[4,64,128]{2,1,0:T(8,128)S(1)}, u32[]{:S(2)}, u32[]{:S(2)}) collective-permute-start(f32[4,64,128]{2,1,0:T(8,128)} %density.1), channel_id=1, source_target_pairs={{0,16},{16,0},{1,17},{17,1},{2,18},{18,2},{3,19},{19,3},{4,20},{20... | collective-permute-start | bytes 393224 | tf_op jit(solution)/shard_map/ppermute | solution.py:843
  3.7 0.0 copy-start
  3.7 1.0 %copy-done = f32[3,4,64,128]{3,2,1,0:T(8,128)S(1)} copy-done((f32[3,4,64,128]{3,2,1,0:T(8,128)S(1)}, f32[3,4,64,128]{3,2,1,0:T(8,128)}, u32[]{:S(2)}) %copy-start) | copy-done | bytes 393240
  4.7 0.0 copy-start.1
  4.7 0.9 %copy-done.1 = s32[4,64,128]{2,1,0:T(8,128)S(1)} copy-done((s32[4,64,128]{2,1,0:T(8,128)S(1)}, s32[4,64,128]{2,1,0:T(8,128)}, u32[]{:S(2)}) %copy-start.1) | copy-done | bytes 131096
  5.6 0.0 copy-start.2
  5.6 0.9 %copy-done.2 = s32[4,64,128]{2,1,0:T(8,128)S(1)} copy-done((s32[4,64,128]{2,1,0:T(8,128)S(1)}, s32[4,64,128]{2,1,0:T(8,128)}, u32[]{:S(2)}) %copy-start.2) | copy-done | bytes 131096
  6.5 0.0 copy-start.3
  6.5 0.9 %copy-done.3 = f32[4,64,128]{2,1,0:T(8,128)S(1)} copy-done((f32[4,64,128]{2,1,0:T(8,128)S(1)}, f32[4,64,128]{2,1,0:T(8,128)}, u32[]{:S(2)}) %copy-start.3) | copy-done | bytes 131096
  7.4 0.1 shard_map.67
  7.4 0.1 collective-permute-start.5
  7.5 0.0 collective-permute-done.other
  7.5 0.1 collective-permute-start.1
  7.6 0.7 %collective-permute-start.2 = (f32[16,8,128]{2,1,0:T(8,128)S(1)}, f32[16,8,128]{2,1,0:T(8,128)S(1)}, u32[]{:S(2)}, u32[]{:S(2)}) collective-permute-start(f32[16,8,128]{2,1,0:T(8,128)S(1)} %get-tuple-element.26), channel_id=1, source_target_pairs={{4,8},{8,4},{5,9},{9,5},{6,10},{10,6},{7,11},{11,7},{20,24},{24,20... | collective-permute-start | bytes 196616 | tf_op jit(solution)/shard_map/ppermute | solution.py:843
  8.3 0.6 collective-permute-done.1.from_a
  8.9 0.0 collective-permute-done.2.from_b
  8.9 0.3 shard_map.69
  9.2 0.7 %collective-permute-start.4 = (f32[224,128]{1,0:T(8,128)S(1)}, f32[224,128]{1,0:T(8,128)S(1)}, u32[]{:S(2)}, u32[]{:S(2)}) collective-permute-start(f32[224,128]{1,0:T(8,128)S(1)} %get-tuple-element.29.strips), channel_id=1, source_target_pairs={{1,2},{2,1},{5,6},{6,5},{9,10},{10,9},{13,14},{14,13},{17,18},{18,... | collective-permute-start | bytes 344072 | tf_op jit(solution)/shard_map/ppermute | solution.py:843
  9.9 4.9 %collective-permute-start.3 = (f32[224,128]{1,0:T(8,128)S(1)}, f32[224,128]{1,0:T(8,128)S(1)}, u32[]{:S(2)}, u32[]{:S(2)}) collective-permute-start(f32[224,128]{1,0:T(8,128)S(1)} %get-tuple-element.29.strips), channel_id=1, source_target_pairs={{0,1},{2,3},{1,0},{3,2},{4,5},{6,7},{5,4},{7,6},{8,9},{10,11},{9,8... | collective-permute-start | bytes 344072 | tf_op jit(solution)/shard_map/ppermute | solution.py:843
  14.8 0.0 collective-permute-done.4.from_b
  14.8 2.8 %collective-permute-done.3.from_a = f32[224,128]{1,0:T(8,128)S(1)} collective-permute-done((f32[224,128]{1,0:T(8,128)S(1)}, f32[224,128]{1,0:T(8,128)S(1)}, u32[]{:S(2)}, u32[]{:S(2)}) %collective-permute-start.3) | collective-permute-done | bytes 114720 | tf_op jit(solution)/shard_map/ppermute | solution.py:843
  17.6 1.0 %shard_map.70 = (f32[8,80,128]{2,1,0:T(8,128)S(1)}, f32[80,128]{1,0:T(8,128)S(1)}, f32[80,128]{1,0:T(8,128)S(1)}, f32[416,128]{1,0:T(8,128)S(1)}, f32[32,1,128]{2,1,0:T(1,128)S(1)}) custom-call(f32[8,80,128]{2,1,0:T(8,128)S(1)} %get-tuple-element.27.window, f32[16,8,128]{2,1,0:T(8,128)S(1)} %get-tuple-element.28.tails, ...), custom_call_target="tpu_custom_call" | custom-call | tf_op jit(solution)/shard_map/pallas_call | solution.py:828
  18.6 1.6 %collective-permute-start.6 = (f32[416,128]{1,0:T(8,128)S(1)}, f32[416,128]{1,0:T(8,128)S(1)}, u32[]{:S(2)}, u32[]{:S(2)}) collective-permute-start(f32[416,128]{1,0:T(8,128)S(1)} %get-tuple-element.34.strip_own), channel_id=1, source_target_pairs={{0,16},{16,0},{1,17},{17,1},{2,18},{18,2},{3,19},{19,3},{4,20},{20... | collective-permute-start | bytes 638984 | tf_op jit(solution)/shard_map/ppermute | solution.py:843
  20.2 14.6 %all_to_all.10.filter_dots = f32[32,1,128]{2,1,0:T(1,128)S(1)} all-to-all(f32[32,1,128]{2,1,0:T(1,128)S(1)} %get-tuple-element.33), channel_id=1, replica_groups=mesh['gx'=2,'gy'=4,'gz'=4] {'gx','gy','gz'}, dimensions={0} | all-to-all | bytes 32768 | tf_op jit(solution)/shard_map/all_to_all | solution.py:875
  34.8 0.0 collective-permute-done.6.strip_other
  34.8 0.0 collective-permute-done.5.node_other
  34.8 13.0 %shard_map.71 = (f32[4,64,128]{2,1,0:T(8,128)}, f32[5,3,4,64,128]{4,3,2,1,0:T(8,128)S(1)}, f32[5,3,64,128]{3,2,1,0:T(8,128)S(1)}, f32[4,64,128]{2,1,0:T(8,128)S(...) custom-call(f32[8,80,128]{2,1,0:T(8,128)S(1)} %get-tuple-element.27.window, ...), custom_call_target="tpu_custom_call" | custom-call | tf_op jit(solution)/shard_map/pallas_call | solution.py:828
  47.9 8.8 %all_to_all.11.dots = f32[32,1,128]{2,1,0:T(1,128)S(1)} all-to-all(f32[32,1,128]{2,1,0:T(1,128)S(1)} %get-tuple-element.36), channel_id=1, replica_groups=mesh['gx'=2,'gy'=4,'gz'=4] {'gx','gy','gz'}, dimensions={0} | all-to-all | bytes 32768 | tf_op jit(solution)/shard_map/all_to_all | solution.py:891
  56.7 1.4 %shard_map.72 = (f32[3,4,64,128]{3,2,1,0:T(8,128)}, f32[3,4,64,128]{3,2,1,0:T(8,128)}) custom-call(f32[32,1,128]{2,1,0:T(1,128)S(1)} %all_to_all.11.dots, f32[5,3,4,64,128]{4,3,2,1,0:T(8,128)S(1)} %get-tuple-element.37.basis, f32[5,3,64,128]{3,2,1,0:T(8,128)S(1)} %get-tuple-element.38.strips, f32[4,64,128]{2,1,0:T(8,128)S(1)} %get-tuple-element.39.scale, ...), custom_call_target="tpu_custom_call" | custom-call | tf_op jit(solution)/shard_map/pallas_call | solution.py:828
  (1 shorter events, 0.0 us)
Async XLA Ops:
  0.6 6.9 %collective-permute-start = (f32[4,64,128]{2,1,0:T(8,128)}, f32[4,64,128]{2,1,0:T(8,128)S(1)}, u32[]{:S(2)}, u32[]{:S(2)}) collective-permute-start(f32[4,64,128]{2,1,0:T(8,128)} %density.1), channel_id=1, source_target_pairs={{0,16},{16,0},{1,17},{17,1},{2,18},{18,2},{3,19},{19,3},{4,20},{20... | collective-permute-start | bytes 393224 | tf_op jit(solution)/shard_map/ppermute | solution.py:843
  3.7 1.0 %copy-start = (f32[3,4,64,128]{3,2,1,0:T(8,128)S(1)}, f32[3,4,64,128]{3,2,1,0:T(8,128)}, u32[]{:S(2)}) copy-start(f32[3,4,64,128]{3,2,1,0:T(8,128)} %load_values.1) | copy-start | bytes 1179652
  4.7 0.9 %copy-start.1 = (s32[4,64,128]{2,1,0:T(8,128)S(1)}, s32[4,64,128]{2,1,0:T(8,128)}, u32[]{:S(2)}) copy-start(s32[4,64,128]{2,1,0:T(8,128)} %fixed.1) | copy-start | bytes 393220
  5.6 0.9 %copy-start.2 = (s32[4,64,128]{2,1,0:T(8,128)S(1)}, s32[4,64,128]{2,1,0:T(8,128)}, u32[]{:S(2)}) copy-start(s32[4,64,128]{2,1,0:T(8,128)} %load_mask.1) | copy-start | bytes 393220
  6.5 0.9 %copy-start.3 = (f32[4,64,128]{2,1,0:T(8,128)S(1)}, f32[4,64,128]{2,1,0:T(8,128)}, u32[]{:S(2)}) copy-start(f32[4,64,128]{2,1,0:T(8,128)} %density.1) | copy-start | bytes 393220
  7.4 27.4 %collective-permute-start.5 = (f32[16,64,128]{2,1,0:T(8,128)S(1)}, f32[16,64,128]{2,1,0:T(8,128)S(1)}, u32[]{:S(2)}, u32[]{:S(2)}) collective-permute-start(f32[16,64,128]{2,1,0:T(8,128)S(1)} %get-tuple-element.24.nodes.node_own), channel_id=1, source_target_pairs={{0,16},{16,0},{1,17},{17,1},{2,18},{18,2},{3,19},{19,3},{4,20},{20... | collective-permute-start | bytes 1572872 | tf_op jit(solution)/shard_map/ppermute | solution.py:843
  7.5 1.3 %collective-permute-start.1 = (f32[16,8,128]{2,1,0:T(8,128)S(1)}, f32[16,8,128]{2,1,0:T(8,128)S(1)}, u32[]{:S(2)}, u32[]{:S(2)}) collective-permute-start(f32[16,8,128]{2,1,0:T(8,128)S(1)} %get-tuple-element.25), channel_id=1, source_target_pairs={{0,4},{8,12},{4,0},{12,8},{1,5},{9,13},{5,1},{13,9},{2,6},{10,14},... | collective-permute-start | bytes 196616 | tf_op jit(solution)/shard_map/ppermute | solution.py:843
  7.6 1.2 %collective-permute-start.2 = (f32[16,8,128]{2,1,0:T(8,128)S(1)}, f32[16,8,128]{2,1,0:T(8,128)S(1)}, u32[]{:S(2)}, u32[]{:S(2)}) collective-permute-start(f32[16,8,128]{2,1,0:T(8,128)S(1)} %get-tuple-element.26), channel_id=1, source_target_pairs={{4,8},{8,4},{5,9},{9,5},{6,10},{10,6},{7,11},{11,7},{20,24},{24,20... | collective-permute-start | bytes 196616 | tf_op jit(solution)/shard_map/ppermute | solution.py:843
  9.2 5.6 %collective-permute-start.4 = (f32[224,128]{1,0:T(8,128)S(1)}, f32[224,128]{1,0:T(8,128)S(1)}, u32[]{:S(2)}, u32[]{:S(2)}) collective-permute-start(f32[224,128]{1,0:T(8,128)S(1)} %get-tuple-element.29.strips), channel_id=1, source_target_pairs={{1,2},{2,1},{5,6},{6,5},{9,10},{10,9},{13,14},{14,13},{17,18},{18,... | collective-permute-start | bytes 344072 | tf_op jit(solution)/shard_map/ppermute | solution.py:843
  9.9 7.7 %collective-permute-start.3 = (f32[224,128]{1,0:T(8,128)S(1)}, f32[224,128]{1,0:T(8,128)S(1)}, u32[]{:S(2)}, u32[]{:S(2)}) collective-permute-start(f32[224,128]{1,0:T(8,128)S(1)} %get-tuple-element.29.strips), channel_id=1, source_target_pairs={{0,1},{2,3},{1,0},{3,2},{4,5},{6,7},{5,4},{7,6},{8,9},{10,11},{9,8... | collective-permute-start | bytes 344072 | tf_op jit(solution)/shard_map/ppermute | solution.py:843
  18.6 16.2 %collective-permute-start.6 = (f32[416,128]{1,0:T(8,128)S(1)}, f32[416,128]{1,0:T(8,128)S(1)}, u32[]{:S(2)}, u32[]{:S(2)}) collective-permute-start(f32[416,128]{1,0:T(8,128)S(1)} %get-tuple-element.34.strip_own), channel_id=1, source_target_pairs={{0,16},{16,0},{1,17},{17,1},{2,18},{18,2},{3,19},{19,3},{4,20},{20... | collective-permute-start | bytes 638984 | tf_op jit(solution)/shard_map/ppermute | solution.py:843

commit v4 on v3

--- a/solution.py
+++ b/solution.py
@@ -445,7 +445,7 @@
 def solve_kernel(
     grid, diagonal, window, first, strip_v, strip_g, filter_dots, node_own, node_other, strip_own, strip_other,
     filtered, fields, strip_fields, scale, strip_scale, dots,
-    basis_0, basis_1, basis_2, basis_3, basis_4, modulus, inverse, free, pairs, kept, carried, near, far,
+    basis_0, basis_1, basis_2, basis_3, basis_4, modulus, inverse, free, pairs_0, pairs_1, kept, carried, near, far,
     s_basis, s_modulus, s_inverse, s_free, s_pairs, s_near, s_far, s_part, s_disp,
 ):
     basis = (basis_0, basis_1, basis_2, basis_3, basis_4)
@@ -622,28 +622,26 @@
         if j < 3:
             strip_pairs()
 
-    def spread_z(c, p, r, disp):
-        ahead = turned(disp, -1, 1)
-        pairs[2 * c, p, r : r + 8] = disp + ahead
-        pairs[2 * c + 1, p, r : r + 8] = ahead - disp
-
-    def close_rows(p):
+    def close_rows(pairs, p):
         for k in range(6):
             pairs[k, p, tall : tall + 1] = pairs[k, p, 0:1]
 
-    for k in range(6):
-        pairs[k, count] = jnp.zeros(pairs.shape[2:], jnp.float32)
+    for pairs in (pairs_0, pairs_1):
+        for k in range(6):
+            pairs[k, count] = jnp.zeros(pairs.shape[2:], jnp.float32)
 
     def start_plane(p, carry):
-        for r in starts:
-            for c in range(3):
-                spread_z(c, p, r, inverse[p, r : r + 8] * basis_0[c, p, r : r + 8])
-        close_rows(p)
+        disp = {(r, c): inverse[p, r : r + 8] * basis_0[c, p, r : r + 8] for r in starts for c in range(3)}
+        ahead = {key: turned(value, -1, 1) for key, value in disp.items()}
+        for (r, c), value in disp.items():
+            pairs_0[2 * c, p, r : r + 8] = value + ahead[r, c]
+            pairs_0[2 * c + 1, p, r : r + 8] = ahead[r, c] - value
+        close_rows(pairs_0, p)
         return carry
 
     lax.fori_loop(0, count, start_plane, 0)
 
-    def along_rows(p, r):
+    def along_rows(pairs, p, r):
         result = []
         for k in range(6):
             now = pairs[k, p, r : r + 8]
@@ -651,76 +649,107 @@
             result.append((now + after, after - now))
         return result
 
+    def elements(pairs, p, r):
+        upper_rows = along_rows(pairs, p + 1, r)
+        u = []
+        for c in range(3):
+            modes = {}
+            for g in range(2):
+                for beta_ in range(2):
+                    k = 2 * (2 * c + g) + beta_
+                    now = kept[k, r : r + 8]
+                    above = upper_rows[2 * c + g][beta_]
+                    if (beta_, g) != (0, 0):
+                        modes[0, beta_, g] = now + above
+                    modes[1, beta_, g] = above - now
+                    kept[k, r : r + 8] = above
+            u.append(modes)
+        f = element_forces(u, modulus[p, r : r + 8])
+        for c in range(3):
+            for g in range(2):
+                t_beta = []
+                for beta_ in range(2):
+                    k = 2 * (2 * c + g) + beta_
+                    diff = f[c][1, beta_, g]
+                    before = carried[k, r : r + 8]
+                    if (beta_, g) == (0, 0):
+                        t_beta.append(before - diff)
+                        carried[k, r : r + 8] = diff
+                    else:
+                        total = f[c][0, beta_, g]
+                        t_beta.append(before + (total - diff))
+                        carried[k, r : r + 8] = total + diff
+                near[2 * c + g, r : r + 8] = t_beta[0] - t_beta[1]
+                far[2 * c + g, r + 8 : r + 16] = t_beta[0] + t_beta[1]
+
+    def close_far():
+        for k in range(6):
+            far[k, 7:8] = far[k, tall + 7 : tall + 8]
+
+    def turn_sums(r):
+        both = []
+        for c in range(3):
+            total = near[2 * c, r : r + 8] + far[2 * c, r + 7 : r + 15]
+            diff = near[2 * c + 1, r : r + 8] + far[2 * c + 1, r + 7 : r + 15]
+            both.append((total - diff, turned(total + diff, 1, 1)))
+        return both
+
+    def new_rows(j, p, r, both):
+        open_nodes = free[p, r : r + 8]
+        inv = inverse[p, r : r + 8]
+        disp = []
+        for c, (here, moved) in enumerate(both):
+            new = open_nodes * (here + moved) - SHIFTS[j] * basis[j][c, p, r : r + 8]
+            basis[j + 1][c, p, r : r + 8] = new
+            if j < 3:
+                disp.append(inv * new)
+        return [(value, turned(value, -1, 1)) for value in disp]
+
+    def put_pairs(pairs, p, r, disp):
+        for c, (value, ahead) in enumerate(disp):
+            pairs[2 * c, p, r : r + 8] = value + ahead
+            pairs[2 * c + 1, p, r : r + 8] = ahead - value
+
     for j in range(4):
+        source, target = (pairs_0, pairs_1) if j % 2 == 0 else (pairs_1, pairs_0)
         low = gx * j
         high = count - 1 - j + gx * (j + 1)
         for r in starts:
-            for k, both in enumerate(along_rows(low, r)):
+            for k, both in enumerate(along_rows(source, low, r)):
                 for beta_ in range(2):
                     kept[2 * k + beta_, r : r + 8] = both[beta_]
                     carried[2 * k + beta_, r : r + 8] = jnp.zeros((8, lanes), jnp.float32)
 
-        def layer(p, state, j=j, low=low):
+        def only_elements(p, state, source=source):
             for r in starts:
-                upper_rows = along_rows(p + 1, r)
-                u = []
-                for c in range(3):
-                    modes = {}
-                    for g in range(2):
-                        for beta_ in range(2):
-                            k = 2 * (2 * c + g) + beta_
-                            now = kept[k, r : r + 8]
-                            above = upper_rows[2 * c + g][beta_]
-                            if (beta_, g) != (0, 0):
-                                modes[0, beta_, g] = now + above
-                            modes[1, beta_, g] = above - now
-                            kept[k, r : r + 8] = above
-                    u.append(modes)
-                f = element_forces(u, modulus[p, r : r + 8])
-                for c in range(3):
-                    for g in range(2):
-                        t_beta = []
-                        for beta_ in range(2):
-                            k = 2 * (2 * c + g) + beta_
-                            diff = f[c][1, beta_, g]
-                            before = carried[k, r : r + 8]
-                            if (beta_, g) == (0, 0):
-                                t_beta.append(before - diff)
-                                carried[k, r : r + 8] = diff
-                            else:
-                                total = f[c][0, beta_, g]
-                                t_beta.append(before + (total - diff))
-                                carried[k, r : r + 8] = total + diff
-                        near[2 * c + g, r : r + 8] = t_beta[0] - t_beta[1]
-                        far[2 * c + g, r + 8 : r + 16] = t_beta[0] + t_beta[1]
-            for k in range(6):
-                far[k, 7:8] = far[k, tall + 7 : tall + 8]
-            @pl.when((p > low) | (gx == 0))
-            def finish():
-                fresh = {}
-                for r in starts:
-                    open_nodes = free[p, r : r + 8]
-                    for c in range(3):
-                        total = near[2 * c, r : r + 8] + far[2 * c, r + 7 : r + 15]
-                        diff = near[2 * c + 1, r : r + 8] + far[2 * c + 1, r + 7 : r + 15]
-                        out = (total - diff) + turned(total + diff, 1, 1)
-                        fresh[r, c] = open_nodes * out - SHIFTS[j] * basis[j][c, p, r : r + 8]
-                for r in starts:
-                    for c in range(3):
-                        basis[j + 1][c, p, r : r + 8] = fresh[r, c]
-                        if j < 3:
-                            fresh[r, c] = inverse[p, r : r + 8] * fresh[r, c]
-                if j < 3:
-                    ahead = {key: turned(value, -1, 1) for key, value in fresh.items()}
-                    for (r, c), value in fresh.items():
-                        pairs[2 * c, p, r : r + 8] = value + ahead[r, c]
-                        pairs[2 * c + 1, p, r : r + 8] = ahead[r, c] - value
-                if j < 3:
-                    close_rows(p)
-
+                elements(source, p, r)
+            close_far()
             return state
 
-        lax.fori_loop(low, high, layer, 0)
+        def layer(p, state, j=j, source=source, target=target):
+            waiting = {0: turn_sums(0)}
+            pending = None
+            for r in starts:
+                if r + 8 < tall:
+                    waiting[r + 8] = turn_sums(r + 8)
+                disp = new_rows(j, p - 1, r, waiting.pop(r))
+                elements(source, p, r)
+                if pending is not None:
+                    put_pairs(target, p - 1, *pending)
+                pending = (r, disp)
+            put_pairs(target, p - 1, *pending)
+            if j < 3:
+                close_rows(target, p - 1)
+            close_far()
+            return state
+
+        lax.fori_loop(low, low + 1 + gx, only_elements, 0)
+        lax.fori_loop(low + 1 + gx, high, layer, 0)
+        for r in starts if j < 3 else range(0, rows, 8):
+            disp = new_rows(j, high - 1, r, turn_sums(r))
+            put_pairs(target, high - 1, r, disp)
+        if j < 3:
+            close_rows(target, high - 1)
 
     order = [(i, k) for i in range(4) for k in range(i, 5)]
     zero = jnp.zeros((8, lanes), jnp.float32)
@@ -883,7 +912,7 @@
         scratch=[
             pltpu.VMEM(shape, f32)
             for shape in (
-                *(((3,) + many,) * 5), many, many, many, (6, count + 1) + taller, (12,) + plane, (12,) + plane, (6,) + plane, (6,) + taller,
+                *(((3,) + many,) * 5), many, many, many, (6, count + 1) + taller, (6, count + 1) + taller, (12,) + plane, (12,) + plane, (6,) + plane, (6,) + taller,
                 (5, 3) + plane, plane, plane, plane, (12,) + taller, (12,) + plane, (12,) + taller, (6,) + plane, (3,) + plane,
             )
         ],

time: 58.4 us -> 58 us (level)
  no operation moved by 1% of the time
where the time goes in v4:
time: 58 us; the launch traced here: 57.8 us
  blocking collectives  23.5 us (41%)
  Pallas kernels  15.5 us (27%)
  starting transfers between devices  11 us (19%)
  local copies, waits for them, and re-layouts  3.71 us (6%)
  waiting for transfers between devices  3.35 us (6%)
  between operations  0.69 us (1%)
    all_to_all x2, blocking collectives, paired_shards(): dots = lax.all_to_all(dots, AXES, 0, 0, tiled=True)  23.5 us
    pallas_call x6, Pallas kernels, call(): pl.pallas_call(kernel, out_shape=tuple((jax.ShapeDtypeStruct(shape, jnp.f...  15.5 us
    ppermute x7, starting transfers between devices, swapped(): return lax.ppermute(value, axis, pairs + [(j, i) for i, j in pairs])  11 us
    unnamed x8, local copies, waits for them, and re-layouts  3.71 us
    ppermute x7, waiting for transfers between devices, swapped(): return lax.ppermute(value, axis, pairs + [(j, i) for i, j in pairs])  3.35 us
  transfers between devices with their start and end apart: 7, of which 2 were waited for; matrix products, arithmetic and copies ran while one was open for 0% of the time, Pallas kernels for 2%

profile of v4, /device:TPU:0, one launch (start us, length us, event | category | flops | bytes accessed | tf_op | source)
XLA Modules:
  0.0 57.8 jit_solution(15899158921324775191)
XLA Ops:
  0.6 3.0 %collective-permute-start = (f32[4,64,128]{2,1,0:T(8,128)}, f32[4,64,128]{2,1,0:T(8,128)S(1)}, u32[]{:S(2)}, u32[]{:S(2)}) collective-permute-start(f32[4,64,128]{2,1,0:T(8,128)} %density.1), channel_id=1, source_target_pairs={{0,16},{16,0},{1,17},{17,1},{2,18},{18,2},{3,19},{19,3},{4,20},{20... | collective-permute-start | bytes 393224 | tf_op jit(solution)/shard_map/ppermute | solution.py:872
  3.7 0.0 copy-start
  3.7 1.0 %copy-done = f32[3,4,64,128]{3,2,1,0:T(8,128)S(1)} copy-done((f32[3,4,64,128]{3,2,1,0:T(8,128)S(1)}, f32[3,4,64,128]{3,2,1,0:T(8,128)}, u32[]{:S(2)}) %copy-start) | copy-done | bytes 393240
  4.7 0.0 copy-start.1
  4.7 0.9 %copy-done.1 = s32[4,64,128]{2,1,0:T(8,128)S(1)} copy-done((s32[4,64,128]{2,1,0:T(8,128)S(1)}, s32[4,64,128]{2,1,0:T(8,128)}, u32[]{:S(2)}) %copy-start.1) | copy-done | bytes 131096
  5.6 0.0 copy-start.2
  5.6 0.9 %copy-done.2 = s32[4,64,128]{2,1,0:T(8,128)S(1)} copy-done((s32[4,64,128]{2,1,0:T(8,128)S(1)}, s32[4,64,128]{2,1,0:T(8,128)}, u32[]{:S(2)}) %copy-start.2) | copy-done | bytes 131096
  6.5 0.0 copy-start.3
  6.5 0.9 %copy-done.3 = f32[4,64,128]{2,1,0:T(8,128)S(1)} copy-done((f32[4,64,128]{2,1,0:T(8,128)S(1)}, f32[4,64,128]{2,1,0:T(8,128)}, u32[]{:S(2)}) %copy-start.3) | copy-done | bytes 131096
  7.4 0.1 shard_map.67
  7.4 0.1 collective-permute-start.5
  7.5 0.0 collective-permute-done.other
  7.5 0.1 collective-permute-start.1
  7.6 0.7 %collective-permute-start.2 = (f32[16,8,128]{2,1,0:T(8,128)S(1)}, f32[16,8,128]{2,1,0:T(8,128)S(1)}, u32[]{:S(2)}, u32[]{:S(2)}) collective-permute-start(f32[16,8,128]{2,1,0:T(8,128)S(1)} %get-tuple-element.26), channel_id=1, source_target_pairs={{4,8},{8,4},{5,9},{9,5},{6,10},{10,6},{7,11},{11,7},{20,24},{24,20... | collective-permute-start | bytes 196616 | tf_op jit(solution)/shard_map/ppermute | solution.py:872
  8.3 0.6 collective-permute-done.1.from_a
  8.9 0.0 collective-permute-done.2.from_b
  8.9 0.3 shard_map.69
  9.2 0.7 %collective-permute-start.4 = (f32[224,128]{1,0:T(8,128)S(1)}, f32[224,128]{1,0:T(8,128)S(1)}, u32[]{:S(2)}, u32[]{:S(2)}) collective-permute-start(f32[224,128]{1,0:T(8,128)S(1)} %get-tuple-element.29.strips), channel_id=1, source_target_pairs={{1,2},{2,1},{5,6},{6,5},{9,10},{10,9},{13,14},{14,13},{17,18},{18,... | collective-permute-start | bytes 344072 | tf_op jit(solution)/shard_map/ppermute | solution.py:872
  9.9 4.9 %collective-permute-start.3 = (f32[224,128]{1,0:T(8,128)S(1)}, f32[224,128]{1,0:T(8,128)S(1)}, u32[]{:S(2)}, u32[]{:S(2)}) collective-permute-start(f32[224,128]{1,0:T(8,128)S(1)} %get-tuple-element.29.strips), channel_id=1, source_target_pairs={{0,1},{2,3},{1,0},{3,2},{4,5},{6,7},{5,4},{7,6},{8,9},{10,11},{9,8... | collective-permute-start | bytes 344072 | tf_op jit(solution)/shard_map/ppermute | solution.py:872
  14.8 0.0 collective-permute-done.4.from_b
  14.8 2.8 %collective-permute-done.3.from_a = f32[224,128]{1,0:T(8,128)S(1)} collective-permute-done((f32[224,128]{1,0:T(8,128)S(1)}, f32[224,128]{1,0:T(8,128)S(1)}, u32[]{:S(2)}, u32[]{:S(2)}) %collective-permute-start.3) | collective-permute-done | bytes 114720 | tf_op jit(solution)/shard_map/ppermute | solution.py:872
  17.6 1.0 %shard_map.70 = (f32[8,80,128]{2,1,0:T(8,128)S(1)}, f32[80,128]{1,0:T(8,128)S(1)}, f32[80,128]{1,0:T(8,128)S(1)}, f32[416,128]{1,0:T(8,128)S(1)}, f32[32,1,128]{2,1,0:T(1,128)S(1)}) custom-call(f32[8,80,128]{2,1,0:T(8,128)S(1)} %get-tuple-element.27.window, f32[16,8,128]{2,1,0:T(8,128)S(1)} %get-tuple-element.28.tails, ...), custom_call_target="tpu_custom_call" | custom-call | tf_op jit(solution)/shard_map/pallas_call | solution.py:857
  18.6 1.6 %collective-permute-start.6 = (f32[416,128]{1,0:T(8,128)S(1)}, f32[416,128]{1,0:T(8,128)S(1)}, u32[]{:S(2)}, u32[]{:S(2)}) collective-permute-start(f32[416,128]{1,0:T(8,128)S(1)} %get-tuple-element.34.strip_own), channel_id=1, source_target_pairs={{0,16},{16,0},{1,17},{17,1},{2,18},{18,2},{3,19},{19,3},{4,20},{20... | collective-permute-start | bytes 638984 | tf_op jit(solution)/shard_map/ppermute | solution.py:872
  20.2 14.6 %all_to_all.10.filter_dots = f32[32,1,128]{2,1,0:T(1,128)S(1)} all-to-all(f32[32,1,128]{2,1,0:T(1,128)S(1)} %get-tuple-element.33), channel_id=1, replica_groups=mesh['gx'=2,'gy'=4,'gz'=4] {'gx','gy','gz'}, dimensions={0} | all-to-all | bytes 32768 | tf_op jit(solution)/shard_map/all_to_all | solution.py:904
  34.8 0.0 collective-permute-done.6.strip_other
  34.8 0.0 collective-permute-done.5.node_other
  34.8 12.6 %shard_map.71 = (f32[4,64,128]{2,1,0:T(8,128)}, f32[5,3,4,64,128]{4,3,2,1,0:T(8,128)S(1)}, f32[5,3,64,128]{3,2,1,0:T(8,128)S(1)}, f32[4,64,128]{2,1,0:T(8,128)S(...) custom-call(f32[8,80,128]{2,1,0:T(8,128)S(1)} %get-tuple-element.27.window, ...), custom_call_target="tpu_custom_call" | custom-call | tf_op jit(solution)/shard_map/pallas_call | solution.py:857
  47.5 8.8 %all_to_all.11.dots = f32[32,1,128]{2,1,0:T(1,128)S(1)} all-to-all(f32[32,1,128]{2,1,0:T(1,128)S(1)} %get-tuple-element.36), channel_id=1, replica_groups=mesh['gx'=2,'gy'=4,'gz'=4] {'gx','gy','gz'}, dimensions={0} | all-to-all | bytes 32768 | tf_op jit(solution)/shard_map/all_to_all | solution.py:920
  56.3 1.4 %shard_map.72 = (f32[3,4,64,128]{3,2,1,0:T(8,128)}, f32[3,4,64,128]{3,2,1,0:T(8,128)}) custom-call(f32[32,1,128]{2,1,0:T(1,128)S(1)} %all_to_all.11.dots, f32[5,3,4,64,128]{4,3,2,1,0:T(8,128)S(1)} %get-tuple-element.37.basis, f32[5,3,64,128]{3,2,1,0:T(8,128)S(1)} %get-tuple-element.38.strips, f32[4,64,128]{2,1,0:T(8,128)S(1)} %get-tuple-element.39.scale, ...), custom_call_target="tpu_custom_call" | custom-call | tf_op jit(solution)/shard_map/pallas_call | solution.py:857
  (1 shorter events, 0.0 us)
Async XLA Ops:
  0.6 6.9 %collective-permute-start = (f32[4,64,128]{2,1,0:T(8,128)}, f32[4,64,128]{2,1,0:T(8,128)S(1)}, u32[]{:S(2)}, u32[]{:S(2)}) collective-permute-start(f32[4,64,128]{2,1,0:T(8,128)} %density.1), channel_id=1, source_target_pairs={{0,16},{16,0},{1,17},{17,1},{2,18},{18,2},{3,19},{19,3},{4,20},{20... | collective-permute-start | bytes 393224 | tf_op jit(solution)/shard_map/ppermute | solution.py:872
  3.7 1.0 %copy-start = (f32[3,4,64,128]{3,2,1,0:T(8,128)S(1)}, f32[3,4,64,128]{3,2,1,0:T(8,128)}, u32[]{:S(2)}) copy-start(f32[3,4,64,128]{3,2,1,0:T(8,128)} %load_values.1) | copy-start | bytes 1179652
  4.7 0.9 %copy-start.1 = (s32[4,64,128]{2,1,0:T(8,128)S(1)}, s32[4,64,128]{2,1,0:T(8,128)}, u32[]{:S(2)}) copy-start(s32[4,64,128]{2,1,0:T(8,128)} %fixed.1) | copy-start | bytes 393220
  5.6 0.9 %copy-start.2 = (s32[4,64,128]{2,1,0:T(8,128)S(1)}, s32[4,64,128]{2,1,0:T(8,128)}, u32[]{:S(2)}) copy-start(s32[4,64,128]{2,1,0:T(8,128)} %load_mask.1) | copy-start | bytes 393220
  6.5 0.9 %copy-start.3 = (f32[4,64,128]{2,1,0:T(8,128)S(1)}, f32[4,64,128]{2,1,0:T(8,128)}, u32[]{:S(2)}) copy-start(f32[4,64,128]{2,1,0:T(8,128)} %density.1) | copy-start | bytes 393220
  7.4 27.4 %collective-permute-start.5 = (f32[16,64,128]{2,1,0:T(8,128)S(1)}, f32[16,64,128]{2,1,0:T(8,128)S(1)}, u32[]{:S(2)}, u32[]{:S(2)}) collective-permute-start(f32[16,64,128]{2,1,0:T(8,128)S(1)} %get-tuple-element.24.nodes.node_own), channel_id=1, source_target_pairs={{0,16},{16,0},{1,17},{17,1},{2,18},{18,2},{3,19},{19,3},{4,20},{20... | collective-permute-start | bytes 1572872 | tf_op jit(solution)/shard_map/ppermute | solution.py:872
  7.5 1.3 %collective-permute-start.1 = (f32[16,8,128]{2,1,0:T(8,128)S(1)}, f32[16,8,128]{2,1,0:T(8,128)S(1)}, u32[]{:S(2)}, u32[]{:S(2)}) collective-permute-start(f32[16,8,128]{2,1,0:T(8,128)S(1)} %get-tuple-element.25), channel_id=1, source_target_pairs={{0,4},{8,12},{4,0},{12,8},{1,5},{9,13},{5,1},{13,9},{2,6},{10,14},... | collective-permute-start | bytes 196616 | tf_op jit(solution)/shard_map/ppermute | solution.py:872
  7.6 1.2 %collective-permute-start.2 = (f32[16,8,128]{2,1,0:T(8,128)S(1)}, f32[16,8,128]{2,1,0:T(8,128)S(1)}, u32[]{:S(2)}, u32[]{:S(2)}) collective-permute-start(f32[16,8,128]{2,1,0:T(8,128)S(1)} %get-tuple-element.26), channel_id=1, source_target_pairs={{4,8},{8,4},{5,9},{9,5},{6,10},{10,6},{7,11},{11,7},{20,24},{24,20... | collective-permute-start | bytes 196616 | tf_op jit(solution)/shard_map/ppermute | solution.py:872
  9.2 5.6 %collective-permute-start.4 = (f32[224,128]{1,0:T(8,128)S(1)}, f32[224,128]{1,0:T(8,128)S(1)}, u32[]{:S(2)}, u32[]{:S(2)}) collective-permute-start(f32[224,128]{1,0:T(8,128)S(1)} %get-tuple-element.29.strips), channel_id=1, source_target_pairs={{1,2},{2,1},{5,6},{6,5},{9,10},{10,9},{13,14},{14,13},{17,18},{18,... | collective-permute-start | bytes 344072 | tf_op jit(solution)/shard_map/ppermute | solution.py:872
  9.9 7.7 %collective-permute-start.3 = (f32[224,128]{1,0:T(8,128)S(1)}, f32[224,128]{1,0:T(8,128)S(1)}, u32[]{:S(2)}, u32[]{:S(2)}) collective-permute-start(f32[224,128]{1,0:T(8,128)S(1)} %get-tuple-element.29.strips), channel_id=1, source_target_pairs={{0,1},{2,3},{1,0},{3,2},{4,5},{6,7},{5,4},{7,6},{8,9},{10,11},{9,8... | collective-permute-start | bytes 344072 | tf_op jit(solution)/shard_map/ppermute | solution.py:872
  18.6 16.2 %collective-permute-start.6 = (f32[416,128]{1,0:T(8,128)S(1)}, f32[416,128]{1,0:T(8,128)S(1)}, u32[]{:S(2)}, u32[]{:S(2)}) collective-permute-start(f32[416,128]{1,0:T(8,128)S(1)} %get-tuple-element.34.strip_own), channel_id=1, source_target_pairs={{0,16},{16,0},{1,17},{17,1},{2,18},{18,2},{3,19},{19,3},{4,20},{20... | collective-permute-start | bytes 638984 | tf_op jit(solution)/shard_map/ppermute | solution.py:872
